TPU v7x, 32 devices: a whole 2x2x4 slice. The times are simulated.
32 devices in a mesh: seq: 8 (over z, x), rep: 4 (over y, core).
Axes of the slice: x: 2, y: 2, z: 4, core: 2. Of those that a mesh axis runs over, the one named last changes fastest.
Arguments:
- tokens: bfloat16 [4096, 1024], P(('seq', 'rep')), may hold values from -40 to 40
- cotangent: bfloat16 [4096, 1024], P(('seq', 'rep')), may hold values from -6 to 6
- lengths: int32 [2], replicated, may hold values from 256 to 2048, as said below
- in_weight: bfloat16 [1, 1024, 3, 1024], P(None, 'seq', None, 'rep'), may hold values from -0.1875 to 0.1875
- in_bias: float32 [1, 3, 1024], replicated, may hold values from -2 to 2
- short_taps: float32 [1, 3, 3, 1024], replicated, may hold values from -1 to 1
- short_bias: float32 [1, 3, 1024], replicated, may hold values from -1.5 to 1.5
- feat_weight: float32 [1, 33, 64], replicated, may hold values from -1 to 1
- feat_bias: float32 [1, 64], replicated, may hold values from -4 to 4
- inner_weight: float32 [1, 64, 64], replicated, may hold values from -0.75 to 0.75
- inner_bias: float32 [1, 64], replicated, may hold values from -3 to 3
- deep_weight: float32 [1, 64, 64], replicated, may hold values from -0.75 to 0.75
- deep_bias: float32 [1, 64], replicated, may hold values from -3 to 3
- sine_freq: float32 [1, 64], replicated, may hold values from 0.5 to 1.5
- kernel_weight: float32 [1, 64, 1024], replicated, may hold values from -0.078125 to 0.078125
- skip_gain: float32 [1, 1024], replicated, may hold values from -4 to 4
- out_weight: bfloat16 [1, 1024, 1024], P(None, 'seq', 'rep'), may hold values from -0.1875 to 0.1875
- out_bias: float32 [1, 1024], replicated, may hold values from -1.5 to 1.5
- norm1_gain: float32 [1, 1024], replicated, may hold values from 0.5 to 1.5
- norm1_shift: float32 [1, 1024], replicated, may hold values from -1.5 to 1.5
- norm2_gain: float32 [1, 1024], replicated, may hold values from 0.5 to 1.5
- norm2_shift: float32 [1, 1024], replicated, may hold values from -1.5 to 1.5
- up_weight: bfloat16 [1, 1024, 4096], P(None, 'seq', 'rep'), may hold values from -0.1875 to 0.1875
- up_bias: float32 [1, 4096], replicated, may hold values from -2 to 2
- down_weight: bfloat16 [1, 1024, 4096], P(None, 'seq', 'rep'), may hold values from -0.125 to 0.125
- down_bias: float32 [1, 1024], replicated, may hold values from -1.5 to 1.5
Outputs:
- layer_out: bfloat16 [4096, 1024], P(('seq', 'rep'))
- grad_tokens: float32 [4096, 1024], P(('seq', 'rep'))
- grad_in_weight: float32 [1, 1024, 3, 1024], P(None, 'seq', None, 'rep')
- grad_in_bias: float32 [1, 3, 1024], replicated
- grad_short_taps: float32 [1, 3, 3, 1024], replicated
- grad_short_bias: float32 [1, 3, 1024], replicated
- grad_feat_weight: float32 [1, 33, 64], replicated
- grad_feat_bias: float32 [1, 64], replicated
- grad_inner_weight: float32 [1, 64, 64], replicated
- grad_inner_bias: float32 [1, 64], replicated
- grad_deep_weight: float32 [1, 64, 64], replicated
- grad_deep_bias: float32 [1, 64], replicated
- grad_sine_freq: float32 [1, 64], replicated
- grad_kernel_weight: float32 [1, 64, 1024], replicated
- grad_skip_gain: float32 [1, 1024], replicated
- grad_out_weight: float32 [1, 1024, 1024], P(None, 'seq', 'rep')
- grad_out_bias: float32 [1, 1024], replicated
- grad_norm1_gain: float32 [1, 1024], replicated
- grad_norm1_shift: float32 [1, 1024], replicated
- grad_norm2_gain: float32 [1, 1024], replicated
- grad_norm2_shift: float32 [1, 1024], replicated
- grad_up_weight: float32 [1, 1024, 4096], P(None, 'seq', 'rep')
- grad_up_bias: float32 [1, 4096], replicated
- grad_down_weight: float32 [1, 1024, 4096], P(None, 'seq', 'rep')
- grad_down_bias: float32 [1, 1024], replicated
Inputs may be any that keep to these rules, and one draw needn't show every extreme that they name: lengths[0] is 2048; lengths[1] lies between 256 and 512.
All inputs are finite; a program needn't handle non-finite values.
Results may differ from a plain program's by a relative error of at most 0.017.
Values may be sent and summed in bfloat16 or wider, within the bound.
No kernel may reach another device: no remote copies, remote signals or barrier semaphores. Data moves between devices by JAX's collectives and lax.ppermute only.
A program may use at most 192 MiB of HBM per device.

v0:
```python
from functools import partial
import math

import jax
import jax.numpy as jnp
import numpy as np
from jax import lax
from jax.experimental import pallas as pl
from jax.experimental.pallas import tpu as pltpu
from jax.sharding import PartitionSpec as P

EPS = 1e-05
HIGH = lax.Precision.HIGHEST
F32 = jnp.float32
B16 = jnp.bfloat16
LANE = 128
HALO = 16
VMEM_BYTES = 48 * 2**20


def swap(values, axis_name, bit):
    size = lax.axis_size(axis_name)
    return lax.ppermute(values, axis_name, [(i, i ^ bit) for i in range(size)])


def gather_rel(rows):
    far = swap(rows, "rep", 2)
    near = swap(rows, "rep", 1)
    diag = swap(far, "rep", 1)
    return jnp.concatenate([rows, near, far, diag], axis=0)


def scatter_rel(part):
    rows = part.shape[0] // 4
    blocks = part.reshape(4, rows, part.shape[1])
    far_in = swap(blocks[3].astype(B16), "rep", 1)
    far_sum = (blocks[2] + far_in.astype(F32)).astype(B16)
    near_in = swap(blocks[1].astype(B16), "rep", 1)
    far_out = swap(far_sum, "rep", 2)
    return blocks[0] + near_in.astype(F32) + far_out.astype(F32)


def ring_order(count):
    if count == 8:
        return [0, 2, 4, 6, 7, 5, 3, 1]
    return list(range(count))


def ring_maps(count):
    order = ring_order(count)
    ahead = [(order[i], order[(i + 1) % count]) for i in range(count)]
    return order, ahead, [(b, a) for a, b in ahead]


def ring_gather(shard):
    count = lax.axis_size("seq")
    if count != 8:
        return lax.all_gather(shard, "seq", axis=0)
    order, ahead, back = ring_maps(count)
    place = jnp.asarray(np.argsort(order), jnp.int32)[lax.axis_index("seq")]
    owners = jnp.asarray(order, jnp.int32)
    full = jnp.zeros((count,) + shard.shape, shard.dtype)

    def put(full, piece, step, lo=0):
        owner = owners[(place + step + count) % count]
        start = (owner, lo) + (0,) * (shard.ndim - 1)
        return lax.dynamic_update_slice(full, piece[None], start)

    full = put(full, shard, 0)
    left = right = shard
    for step in range(1, count // 2):
        left = lax.ppermute(left, "seq", ahead)
        right = lax.ppermute(right, "seq", back)
        full = put(full, left, -step)
        full = put(full, right, step)
    half = shard.shape[0] // 2
    left = lax.ppermute(left[:half], "seq", ahead)
    right = lax.ppermute(right[half:], "seq", back)
    full = put(full, left, -(count // 2))
    full = put(full, right, count // 2, half)
    return full


def ring_scatter(term):
    count = lax.axis_size("seq")
    if count != 8:
        return lax.psum_scatter(term, "seq", scatter_dimension=0, tiled=True).astype(F32)
    order, ahead, back = ring_maps(count)
    place = jnp.asarray(np.argsort(order), jnp.int32)[lax.axis_index("seq")]
    owners = jnp.asarray(order, jnp.int32)
    rows = term.shape[0] // count
    half = rows // 2

    def mine(step, lo):
        owner = owners[(place + step + 2 * count) % count]
        return lax.dynamic_slice_in_dim(term, owner * rows + lo, half, 0)

    left, right = mine(-1, 0), mine(1, half)
    for step in range(2, count + 1):
        left = lax.ppermute(left, "seq", ahead).astype(F32) + mine(-step, 0).astype(F32)
        right = lax.ppermute(right, "seq", back).astype(F32) + mine(step, half).astype(F32)
        if step < count:
            left, right = left.astype(B16), right.astype(B16)
    return jnp.concatenate([left, right], axis=0)


def halve_scatter(term):
    count = lax.axis_size("seq")
    bits = count.bit_length() - 1
    seq = lax.axis_index("seq")
    rows = term.shape[0] // count
    half = rows // 2
    split = term.reshape((2,) * bits + (2, half, term.shape[1]))
    results = []
    for part, order in enumerate(([0] + list(range(bits - 1, 0, -1)), list(range(bits - 1, -1, -1)))):
        value = lax.index_in_dim(split, part, bits, keepdims=False)
        left = list(range(bits - 1, -1, -1))
        for bit in order:
            at = left.index(bit)
            on = (seq >> bit) & 1
            keep = lax.dynamic_index_in_dim(value, on, at, keepdims=False)
            give = lax.dynamic_index_in_dim(value, 1 - on, at, keepdims=False)
            value = keep.astype(F32) + swap(give, "seq", 1 << bit).astype(F32)
            left.remove(bit)
            if left:
                value = value.astype(B16)
        results.append(value)
    return jnp.concatenate(results, axis=0)


def spread_gather(shard):
    count = lax.axis_size("seq")
    copies = jnp.broadcast_to(shard[None], (count,) + shard.shape)
    full = lax.all_to_all(copies, "seq", 0, 0, tiled=True)
    return full.reshape((count * shard.shape[0],) + shard.shape[1:])


def shift_seq(values, step):
    count = lax.axis_size("seq")
    return lax.ppermute(values, "seq", [(i, (i + step) % count) for i in range(count)])


def unmix(values, axis, index):
    size, bit = values.shape[axis], 1
    while bit < size:
        cut = values.shape[:axis] + (size // (2 * bit), 2, bit) + values.shape[axis + 1 :]
        split = values.reshape(cut)
        values = jnp.where((index // bit) % 2 == 1, jnp.flip(split, axis + 1), split).reshape(values.shape)
        bit *= 2
    return values


def sync_small(total, group, own):
    n_seq, n_rep = lax.axis_size("seq"), lax.axis_size("rep")
    group_list, own_list = [group], [own]
    for axis_name, size in (("seq", n_seq), ("rep", n_rep)):
        bit = 1
        while bit < size:
            parts = [total] + group_list + own_list
            sizes = np.cumsum([0] + [p.shape[0] for p in parts])
            came = swap(jnp.concatenate(parts, axis=0), axis_name, bit)
            came = [came[a:b] for a, b in zip(sizes[:-1], sizes[1:])]
            total = total + came[0]
            count = len(group_list)
            if axis_name == "seq":
                group_list = [group_list[0] + came[1]]
            else:
                group_list = group_list + came[1 : 1 + count]
            own_list = own_list + came[1 + count :]
            bit *= 2
    groups = unmix(jnp.stack(group_list), 0, lax.axis_index("rep"))
    owns = jnp.stack(own_list).reshape((n_rep, n_seq) + own.shape)
    owns = unmix(unmix(owns, 0, lax.axis_index("rep")), 1, lax.axis_index("seq"))
    return total, groups, owns


def layer_norm(rows, gain, shift):
    row_mean = jnp.mean(rows, axis=-1, keepdims=True)
    centred = rows - row_mean
    variance = jnp.mean(centred * centred, axis=-1, keepdims=True)
    inverse = lax.rsqrt(variance + EPS)
    normed = centred * inverse
    return (normed * gain + shift, normed, inverse)


def norm_back(grad_rows, normed, inverse, gain):
    scaled = grad_rows * gain
    mean_one = jnp.mean(scaled, axis=-1, keepdims=True)
    mean_two = jnp.mean(scaled * normed, axis=-1, keepdims=True)
    grad_in = inverse * (scaled - mean_one - normed * mean_two)
    return (grad_in, jnp.sum(grad_rows * normed, axis=0), jnp.sum(grad_rows, axis=0))


def features(length, feat_count):
    ramp_unit = jnp.linspace(0.0, 1.0, length, dtype=F32)
    angles = jnp.arange(length, dtype=F32)[:, None] * (2.0 * math.pi / length)
    band_freqs = jnp.linspace(
        0.0001, (feat_count - 1) // 2 - 1.0, (feat_count - 1) // 2, dtype=F32
    )[None, :]
    phase_grid = band_freqs * angles
    grid_out = jnp.concatenate(
        [ramp_unit[:, None], jnp.cos(phase_grid), -jnp.sin(phase_grid)], axis=1
    )
    return (grid_out, ramp_unit)


def filter_columns(
    feature_grid,
    ramp_unit,
    start_chan,
    chan_count,
    model_width,
    feat_weight,
    feat_bias,
    inner_weight,
    inner_bias,
    deep_weight,
    deep_bias,
    sine_freq,
    columns,
):
    freq = sine_freq[:, None]

    def layer(weight, bias, below):
        grown = lax.dot_general(weight, below, (((0,), (0,)), ((), ())), precision=HIGH)
        return jnp.sin(freq * (grown + bias[:, None]))

    hidden = layer(feat_weight, feat_bias, feature_grid.T)
    hidden = layer(inner_weight, inner_bias, hidden)
    hidden = layer(deep_weight, deep_bias, hidden)
    deltas = jnp.abs(
        jnp.linspace(math.log(0.01) / 0.3, math.log(0.01) / 1.5, model_width, dtype=F32)
    )
    local_rates = lax.dynamic_slice_in_dim(deltas, start_chan, chan_count)
    return lax.dot_general(
        columns, hidden, (((0,), (0,)), ((), ())), precision=HIGH
    ) * jnp.exp(-ramp_unit[None, :] * local_rates[:, None])


def sin_cos(x):
    turns = jnp.floor(x * (1.0 / math.pi) + 0.5)
    r = x - turns * 3.140625
    r = r - turns * 9.67502593994140625e-4
    r = r - turns * 1.509957990978376432e-7
    sign = 1.0 - 2.0 * (turns - 2.0 * jnp.floor(turns * 0.5))
    q = r * r
    sin = r + r * q * (
        -1.6666666666e-1
        + q * (8.3333333e-3 + q * (-1.98412698e-4 + q * (2.7557319e-6 + q * -2.505210838e-8)))
    )
    cos = 1.0 + q * (
        -0.5
        + q * (4.16666666e-2 + q * (-1.3888888e-3 + q * (2.48015873e-5 + q * (-2.75573192e-7 + q * 2.0876757e-9))))
    )
    return sin * sign, cos * sign


def dot_high(left, right, dims):
    return lax.dot_general(left, right, (dims, ((), ())), precision=HIGH, preferred_element_type=F32)


def filter_forward_kernel(
    grid_ref, ramp_ref, rate_ref, w1_ref, w2_ref, w3_ref, small_ref, columns_ref, twist_ref, hi_ref, lo_ref,
    spec_ref, sin_ref, cos_ref, z_ref
):
    blocks, length = twist_ref.shape[0], twist_ref.shape[3]
    freq = small_ref[:, 3:4]
    below = grid_ref[...]
    for i, w_ref in enumerate((w1_ref, w2_ref, w3_ref)):
        grown = dot_high(w_ref[...].T, below, ((1,), (0,)))
        sin, cos = sin_cos(freq * (grown + small_ref[:, i : i + 1]))
        sin_ref[i] = sin
        cos_ref[i] = cos
        below = sin
    kern = dot_high(columns_ref[...].T, below, ((1,), (0,))) * jnp.exp(-rate_ref[...] * ramp_ref[...])
    cut = [kern[:, b * length : (b + 1) * length] for b in range(blocks)]
    turn_rows(cut, twist_ref, z_ref, 0, blocks)
    spec_ref[...] = dot_split(z_ref[...], hi_ref[...], lo_ref[...], ((1,), (0,)))


def filter_backward_kernel(
    gk_ref, grid_ref, ramp_ref, rate_ref, w1_ref, w2_ref, w3_ref, small_ref, columns_ref, sin_ref, cos_ref,
    gc_ref, g1_ref, g2_ref, g3_ref, gsmall_ref
):
    freq = small_ref[:, 3:4]
    gk = jnp.concatenate([gk_ref[b] for b in range(gk_ref.shape[0])], axis=1)
    gk = gk * jnp.exp(-rate_ref[...] * ramp_ref[...])
    last = ((1,), (1,))
    gc_ref[...] = dot_high(sin_ref[2], gk, last)
    grad = dot_high(columns_ref[...], gk, ((1,), (0,)))
    gfreq = jnp.zeros(freq.shape, F32)
    gbias = [None] * 3
    for i, w_ref, g_ref in ((2, w3_ref, g3_ref), (1, w2_ref, g2_ref), (0, w1_ref, g1_ref)):
        turn = grad * cos_ref[i]
        below = sin_ref[i - 1] if i else grid_ref[...]
        raw = dot_high(turn, below, last)
        total = jnp.sum(turn, axis=1, keepdims=True)
        g_ref[...] = raw * freq
        gbias[i] = total * freq
        gfreq = gfreq + jnp.sum(raw * w_ref[...].T, axis=1, keepdims=True) + total * small_ref[:, i : i + 1]
        if i:
            grad = dot_high(w_ref[...], turn * freq, ((1,), (0,)))
    gsmall_ref[...] = jnp.concatenate(gbias + [gfreq], axis=1)


def feature_table(length, feat_count):
    ramp = np.linspace(0.0, 1.0, length, dtype=np.float32)
    angles = np.arange(length, dtype=np.float32)[:, None] * np.float32(2.0 * math.pi / length)
    half = (feat_count - 1) // 2
    bands = np.linspace(0.0001, half - 1.0, half, dtype=np.float32)[None, :]
    phase = (bands * angles).astype(np.float64)
    table = np.concatenate([ramp[:, None], np.cos(phase), -np.sin(phase)], axis=1)
    return np.ascontiguousarray(table.T).astype(np.float32), ramp[None, :]


def decay_rates(model):
    return np.abs(
        np.linspace(math.log(0.01) / 0.3, math.log(0.01) / 1.5, model, dtype=np.float32)
    )[:, None]


def transform_tables(blocks, length):
    time = np.arange(blocks * length).reshape(blocks, 1, length)
    cls = np.arange(blocks).reshape(1, blocks, 1)
    period = 4 * blocks * length
    turn = (time * (2 * cls + 1)) % period * (2.0 * np.pi / period)
    twist = np.stack([np.cos(turn), -np.sin(turn)], axis=2).astype(np.float32)
    step = np.arange(length)
    turn = (step[:, None] * step[None, :]) % length * (2.0 * np.pi / length)
    cos, sin = np.cos(turn), np.sin(turn)
    table = np.block([[cos, -sin], [sin, cos]]).astype(np.float32)
    return twist, table


def split_table(table):
    hi = table.astype(B16)
    return jnp.asarray(hi), jnp.asarray((table - hi.astype(np.float32)).astype(B16))


def spectrum_of(signal, twist, table):
    turned = jnp.einsum("bqzl,brl->qrzl", twist[: signal.shape[0]], signal, precision=HIGH)
    flat = turned.reshape(turned.shape[:2] + (-1,))
    return jnp.einsum("qrk,kf->qrf", flat, table, precision=HIGH)


def signal_of(spectrum, twist, table):
    blocks, length = twist.shape[0], twist.shape[3]
    turned = jnp.einsum("qrf,kf->qrk", spectrum, table, precision=HIGH)
    turned = turned.reshape(turned.shape[:2] + (2, length))
    return jnp.einsum("bqzl,qrzl->brl", twist, turned, precision=HIGH) * (1.0 / (blocks * length))


def times(left, right, conj_right):
    half = left.shape[-1] // 2
    lr, li = left[..., :half], left[..., half:]
    rr, ri = right[..., :half], right[..., half:]
    if conj_right:
        return jnp.concatenate([lr * rr + li * ri, li * rr - lr * ri], axis=-1)
    return jnp.concatenate([lr * rr - li * ri, lr * ri + li * rr], axis=-1)


def dot_split(values, hi, lo, dims):
    top = values.astype(B16)
    rest = (values - top.astype(F32)).astype(B16)
    dot = partial(lax.dot_general, dimension_numbers=(dims, ((), ())), preferred_element_type=F32)
    return dot(top, hi) + dot(rest, hi) + dot(top, lo)


def turn_rows(blocks_in, twist_ref, z_ref, base, classes):
    rows, length = blocks_in[0].shape
    for q in range(classes):
        for z in range(2):
            acc = None
            for b, block in enumerate(blocks_in):
                term = block * twist_ref[b, q, z : z + 1]
                acc = term if acc is None else acc + term
            z_ref[base + q * rows : base + (q + 1) * rows, z * length : (z + 1) * length] = acc


def back_rows(w, base, rows, block, twist_ref, classes):
    length = w.shape[1] // 2
    acc = None
    for q in range(classes):
        lo, hi = base + q * rows, base + (q + 1) * rows
        for z in range(2):
            term = w[lo:hi, z * length : (z + 1) * length] * twist_ref[block, q, z : z + 1]
            acc = term if acc is None else acc + term
    return acc * (1.0 / (classes * length))


def conv_forward_kernel(short_blocks, x_ref, kern_ref, twist_ref, hi_ref, lo_ref, skip_ref, out_ref, spec_ref, z_ref):
    blocks = twist_ref.shape[0]
    rows = x_ref.shape[1]
    span = blocks * rows
    first = [x_ref[b].astype(F32) for b in range(blocks)]
    second = [x_ref[blocks + b].astype(F32) for b in range(short_blocks)]
    turn_rows(first, twist_ref, z_ref, 0, blocks)
    turn_rows(second, twist_ref, z_ref, span, blocks)
    spec = dot_split(z_ref[...], hi_ref[...], lo_ref[...], ((1,), (0,)))
    spec_ref[...] = spec
    kern = kern_ref[...]
    prod = jnp.concatenate([times(spec[:span], kern, False), times(spec[span:], kern, False)], axis=0)
    w = dot_split(prod, hi_ref[...], lo_ref[...], ((1,), (1,)))
    skip = skip_ref[...]
    for b in range(blocks):
        out_ref[b] = (back_rows(w, 0, rows, b, twist_ref, blocks) + skip * first[b]).astype(B16)
        acc = back_rows(w, span, rows, b, twist_ref, blocks)
        if b < short_blocks:
            acc = acc + skip * second[b]
        out_ref[blocks + b] = acc.astype(B16)


def conv_backward_kernel(
    short_blocks, g_ref, spec_ref, kern_ref, twist_ref, hi_ref, lo_ref, skip_ref, out_ref, grad_kern_ref, z_ref, p_ref
):
    blocks = twist_ref.shape[0]
    rows = g_ref.shape[1]
    span = blocks * rows
    first = [g_ref[b].astype(F32) for b in range(blocks)]
    second = [g_ref[blocks + b].astype(F32) for b in range(short_blocks)]
    turn_rows(first, twist_ref, z_ref, 0, blocks)
    turn_rows(second, twist_ref, z_ref, span, blocks)
    grad = dot_split(z_ref[...], hi_ref[...], lo_ref[...], ((1,), (0,)))
    kern = kern_ref[...]
    p_ref[0:span] = times(grad[:span], kern, True)
    p_ref[span : 2 * span] = times(grad[span:], kern, True)
    p_ref[2 * span :] = times(grad[:span], spec_ref[0:span], True) + times(
        grad[span:], spec_ref[span:], True
    )
    w = dot_split(p_ref[...], hi_ref[...], lo_ref[...], ((1,), (1,)))
    skip = skip_ref[...]
    for b in range(blocks):
        out_ref[b] = (back_rows(w, 0, rows, b, twist_ref, blocks) + skip * first[b]).astype(B16)
        if b < short_blocks:
            acc = back_rows(w, span, rows, b, twist_ref, blocks) + skip * second[b]
            out_ref[blocks + b] = acc.astype(B16)
        else:
            out_ref[blocks + b] = jnp.zeros(out_ref.shape[1:], B16)
        grad_kern_ref[b] = back_rows(w, 2 * span, rows, b, twist_ref, blocks)


def conv_forward(received, kern_spec, twist, table, skip_local):
    blocks, rows, length = received.shape[0] // 2, received.shape[1], received.shape[2]
    short_blocks = -(-blocks // 4)
    skip = skip_local[:, None]
    if blocks != 4:
        x = received.astype(F32)
        spec = jnp.concatenate(
            [
                spectrum_of(x[:blocks], twist, table),
                spectrum_of(x[blocks : blocks + short_blocks], twist, table),
            ],
            axis=0,
        )
        kern = jnp.concatenate([kern_spec, kern_spec], axis=0)
        prod = times(spec, kern, False)
        out = jnp.concatenate(
            [signal_of(prod[:blocks], twist, table), signal_of(prod[blocks:], twist, table)], axis=0
        )
        return ((out + skip * x).astype(B16), spec)
    hi, lo = split_table(table)
    height = 2 * blocks * rows
    out, spec = pl.pallas_call(
        partial(conv_forward_kernel, short_blocks),
        out_shape=(
            jax.ShapeDtypeStruct(received.shape, B16),
            jax.ShapeDtypeStruct((height, 2 * length), F32),
        ),
        scratch_shapes=[pltpu.VMEM((height, 2 * length), F32)],
        compiler_params=pltpu.CompilerParams(vmem_limit_bytes=VMEM_BYTES),
        name="conv_forward",
    )(received, kern_spec.reshape(blocks * rows, 2 * length), twist, hi, lo, skip)
    return out, spec


def conv_backward(grads, spec, kern_spec, twist, table, skip_local):
    blocks, rows, length = grads.shape[0] // 2, grads.shape[1], grads.shape[2]
    short_blocks = -(-blocks // 4)
    skip = skip_local[:, None]
    if blocks != 4:
        g = grads.astype(F32)
        first = spectrum_of(g[:blocks], twist, table)
        second = spectrum_of(g[blocks : blocks + short_blocks], twist, table)
        one = signal_of(times(first, kern_spec, True), twist, table)
        two = signal_of(times(second, kern_spec, True), twist, table)
        cross = times(first, spec[:blocks], True) + times(second, spec[blocks:], True)
        out = jnp.concatenate([one, two], axis=0) + skip * g
        return (out.astype(B16), signal_of(cross, twist, table))
    hi, lo = split_table(table)
    span = blocks * rows
    out, grad_kern = pl.pallas_call(
        partial(conv_backward_kernel, short_blocks),
        out_shape=(
            jax.ShapeDtypeStruct(grads.shape, B16),
            jax.ShapeDtypeStruct((blocks, rows, length), F32),
        ),
        scratch_shapes=[
            pltpu.VMEM((2 * span, 2 * length), F32),
            pltpu.VMEM((3 * span, 2 * length), F32),
        ],
        compiler_params=pltpu.CompilerParams(vmem_limit_bytes=VMEM_BYTES),
        name="conv_backward",
    )(grads, spec, kern_spec.reshape(span, 2 * length), twist, hi, lo, skip)
    return out, grad_kern


def in_order(ref, rep, lead=()):
    count = ref.shape[-1] // LANE
    return [
        ref[lead + (slice(None), pl.ds(pl.multiple_of((rep ^ j) * LANE, LANE), LANE))]
        for j in range(count)
    ]


def put_rel(ref, rep, values, lead=()):
    for j in range(ref.shape[-1] // LANE):
        ref[lead + (slice(None), pl.ds(pl.multiple_of((rep ^ j) * LANE, LANE), LANE))] = values[
            :, j * LANE : (j + 1) * LANE
        ]


def extended(proj_ref, halo_ref, exists, rep, p):
    blocks = [halo_ref[p, :, :LANE]] + in_order(proj_ref, rep, (p,)) + [halo_ref[p, :, LANE:]]
    return jnp.concatenate(blocks, axis=1).astype(F32) * exists


def short_of(ext, col_ref, p):
    return (
        col_ref[:, p : p + 1] * pltpu.roll(ext, 2, 1)
        + col_ref[:, 3 + p : 4 + p] * pltpu.roll(ext, 1, 1)
        + col_ref[:, 6 + p : 7 + p] * ext
        + col_ref[:, 9 + p : 10 + p]
    )


def gate_kernel(rep_ref, proj_ref, halo_ref, col_ref, mask_ref, out_ref):
    rep = rep_ref[0]
    mask, exists = mask_ref[0:1], mask_ref[1:2]
    gate_in = short_of(extended(proj_ref, halo_ref, exists, rep, 1), col_ref, 1)
    values = short_of(extended(proj_ref, halo_ref, exists, rep, 2), col_ref, 2)
    gated = values * gate_in * mask
    out_ref[...] = gated[:, LANE:-LANE].astype(B16)


def output_kernel(rep_ref, proj_ref, halo_ref, col_ref, mask_ref, mixed_ref, out_ref):
    rep = rep_ref[0]
    gate_out = short_of(extended(proj_ref, halo_ref, mask_ref[1:2], rep, 0), col_ref, 0)
    put_rel(out_ref, rep, (gate_out[:, LANE:-LANE] * mixed_ref[...].astype(F32)).astype(B16))


def grad_mix_kernel(rep_ref, proj_ref, halo_ref, col_ref, mask_ref, mixed_ref, gy_ref, out_ref, first_ref):
    rep = rep_ref[0]
    gate_out = short_of(extended(proj_ref, halo_ref, mask_ref[1:2], rep, 0), col_ref, 0)
    gy = jnp.concatenate(in_order(gy_ref, rep), axis=1).astype(F32)
    out_ref[...] = (gy * gate_out[:, LANE:-LANE]).astype(B16)
    first_ref[...] = gy[:, :LANE] * mixed_ref[:, :LANE].astype(F32)


def grad_proj_kernel(
    rep_ref, proj_ref, halo_ref, col_ref, mask_ref, mixed_ref, gy_ref, ggated_ref, gnext_ref, onext_ref, out_ref, sum_ref
):
    rep = rep_ref[0]
    mask, exists = mask_ref[0:1], mask_ref[1:2]
    size = mask_ref.shape[1]
    mid = slice(LANE, size - LANE)
    gy = jnp.concatenate(in_order(gy_ref, rep), axis=1).astype(F32)
    zero = jnp.zeros((gy.shape[0], LANE), F32)
    next_on = exists[:, size - LANE :]
    ext = [extended(proj_ref, halo_ref, exists, rep, p) for p in range(3)]
    short = [short_of(ext[p], col_ref, p) for p in range(3)]
    ggated = jnp.concatenate(
        [zero, ggated_ref[...].astype(F32), gnext_ref[...].astype(F32) * next_on], axis=1
    )
    ggated = ggated * mask
    gout = gy * mixed_ref[...].astype(F32)
    gshort = [
        jnp.concatenate([zero, gout, onext_ref[...] * next_on], axis=1),
        ggated * short[2],
        ggated * short[1],
    ]
    gated = short[2][:, mid] * short[1][:, mid] * mask[:, mid]
    sums = [jnp.sum(gy * short[0][:, mid] * gated, axis=1, keepdims=True)]
    for p in range(3):
        mine = gshort[p][:, mid]
        sums.append(jnp.sum(mine, axis=1, keepdims=True))
        sums.append(jnp.sum(mine * ext[p][:, mid], axis=1, keepdims=True))
        sums.append(jnp.sum(mine * pltpu.roll(ext[p], 1, 1)[:, mid], axis=1, keepdims=True))
        sums.append(jnp.sum(mine * pltpu.roll(ext[p], 2, 1)[:, mid], axis=1, keepdims=True))
        gproj = (
            col_ref[:, 6 + p : 7 + p] * gshort[p]
            + col_ref[:, 3 + p : 4 + p] * pltpu.roll(gshort[p], size - 1, 1)
            + col_ref[:, p : p + 1] * pltpu.roll(gshort[p], size - 2, 1)
        )[:, mid].astype(B16)
        sums.append(jnp.sum(gproj.astype(F32), axis=1, keepdims=True))
        put_rel(out_ref, rep, gproj, (p,))
    sum_ref[...] = jnp.concatenate(sums, axis=1)


def token_call(kernel, name, arrays, outs):
    step = 64

    def spec(shape, cut):
        if not cut:
            return pl.BlockSpec(shape, lambda i: (0,) * len(shape))
        if len(shape) == 3:
            return pl.BlockSpec((shape[0], step, shape[2]), lambda i: (0, i, 0))
        return pl.BlockSpec((step, shape[1]), lambda i: (i, 0))

    width = outs[0].shape[-2]
    return pl.pallas_call(
        kernel,
        grid=(width // step,),
        in_specs=[pl.BlockSpec(memory_space=pltpu.SMEM)] + [spec(a.shape, cut) for a, cut in arrays[1:]],
        out_specs=[spec(o.shape, True) for o in outs],
        out_shape=outs,
        compiler_params=pltpu.CompilerParams(vmem_limit_bytes=VMEM_BYTES),
        name=name,
    )(*[a for a, _ in arrays])


def rows128(values):
    flat = values.reshape(-1)
    return jnp.pad(flat, (0, -flat.shape[0] % 1024)).reshape(-1, 128)


def per_device(
    tokens,
    cotangent,
    lengths,
    in_weight,
    in_bias,
    short_taps,
    short_bias,
    feat_weight,
    feat_bias,
    inner_weight,
    inner_bias,
    deep_weight,
    deep_bias,
    sine_freq,
    kernel_weight,
    skip_gain,
    out_weight,
    out_bias,
    norm1_gain,
    norm1_shift,
    norm2_gain,
    norm2_shift,
    up_weight,
    up_bias,
    down_weight,
    down_bias,
):
    n_seq, n_rep = lax.axis_size("seq"), lax.axis_size("rep")
    seq, rep = lax.axis_index("seq"), lax.axis_index("rep")
    tok_rows, model = tokens.shape
    group = tok_rows * n_rep
    blocks = n_seq // 2
    seq_len = blocks * group
    chan = model // (n_seq * n_rep)
    width = model // n_rep
    hidden = up_weight.shape[2]
    block_start = rep * width
    chan_start = block_start + seq * chan
    rep_scalar = jnp.reshape(rep, (1,)).astype(jnp.int32)

    item_len = jnp.where(seq // blocks == 0, lengths[0], lengths[1])
    at = (seq % blocks) * group
    row_mask = (at + rep * tok_rows + jnp.arange(tok_rows, dtype=jnp.int32) < item_len).astype(F32)[:, None]
    position = at - LANE + jnp.arange(group + 2 * LANE, dtype=jnp.int32)
    mask_ext = jnp.stack([position < item_len, (position >= 0) & (position < seq_len)]).astype(F32)
    mask_ext = jnp.pad(mask_ext, ((0, 6), (0, 0)))

    full_in = ring_gather(in_weight[0]).reshape(model, 3, width)
    full_out = spread_gather(out_weight[0])
    full_up = lax.all_gather(up_weight[0], "seq", axis=0, tiled=True)
    full_down = lax.all_gather(down_weight[0], "seq", axis=0, tiled=True)

    residual = tokens.astype(F32)
    normed_one, unit_one, scale_one = layer_norm(residual, norm1_gain[0], norm1_shift[0])
    normed_one = normed_one.astype(B16)
    rows_one = gather_rel(normed_one)
    rel = rows_one.reshape(n_rep, tok_rows, model)
    last_rows = lax.dynamic_index_in_dim(rel, rep ^ (n_rep - 1), 0, False)[-HALO:]
    first_rows = lax.dynamic_index_in_dim(rel, rep, 0, False)[:HALO]
    before = shift_seq(last_rows, 1)
    after = shift_seq(first_rows, -1)
    gap = jnp.zeros((LANE - HALO, model), B16)
    halo_rows = jnp.concatenate([gap, before, after, gap], axis=0)
    proj_bias = lax.dynamic_slice_in_dim(in_bias[0], block_start, width, 1)[:, :, None]

    def project(rows):
        return (
            jnp.einsum("td,dpc->pct", rows, full_in, preferred_element_type=F32) + proj_bias
        ).astype(B16)

    proj = project(rows_one)
    halo = project(halo_rows)

    tap_cols = lax.dynamic_slice_in_dim(short_taps[0], block_start, width, 2).reshape(9, width)
    bias_cols = lax.dynamic_slice_in_dim(short_bias[0], block_start, width, 1)
    cols = jnp.pad(jnp.concatenate([tap_cols, bias_cols], axis=0), ((0, 4), (0, 0))).T
    common = [(rep_scalar, True), (proj, True), (halo, True), (cols, True), (mask_ext, False)]
    flat_shape = jax.ShapeDtypeStruct((width, group), B16)
    (gated,) = token_call(gate_kernel, "gate", common, [flat_shape])
    received = lax.all_to_all(gated.reshape(n_seq, chan, group), "seq", 0, 0, tiled=True)

    skip_local = lax.dynamic_slice_in_dim(skip_gain[0], chan_start, chan, 0)
    columns = lax.dynamic_slice_in_dim(kernel_weight[0], chan_start, chan, 1)
    twist, table = transform_tables(blocks, group)
    nets = (feat_weight[0], inner_weight[0], deep_weight[0])
    if blocks == 4:
        grid, ramp = feature_table(seq_len, feat_weight.shape[1])
        rates = lax.dynamic_slice_in_dim(jnp.asarray(decay_rates(model)), chan_start, chan, 0)
        smalls = jnp.concatenate([feat_bias, inner_bias, deep_bias, sine_freq], axis=0).T
        filt = smalls.shape[0]
        hi, lo = split_table(table)
        kern_spec, sines, cosines = pl.pallas_call(
            filter_forward_kernel,
            out_shape=(
                jax.ShapeDtypeStruct((blocks * chan, 2 * group), F32),
                jax.ShapeDtypeStruct((3, filt, seq_len), F32),
                jax.ShapeDtypeStruct((3, filt, seq_len), F32),
            ),
            scratch_shapes=[pltpu.VMEM((blocks * chan, 2 * group), F32)],
            compiler_params=pltpu.CompilerParams(vmem_limit_bytes=VMEM_BYTES),
            cost_estimate=pl.CostEstimate(flops=10**6, bytes_accessed=10**6, transcendentals=0),
            name="filter_forward",
        )(grid, ramp, rates, *nets, smalls, columns, twist, hi, lo)
        kern_spec = kern_spec.reshape(blocks, chan, 2 * group)

        def kernel_pull(grad_kernel):
            shapes = [columns.shape] + [w.shape[::-1] for w in nets] + [smalls.shape]
            gcols, g1, g2, g3, gsmalls = pl.pallas_call(
                filter_backward_kernel,
                out_shape=tuple(jax.ShapeDtypeStruct(shape, F32) for shape in shapes),
                compiler_params=pltpu.CompilerParams(vmem_limit_bytes=VMEM_BYTES),
                cost_estimate=pl.CostEstimate(flops=10**6, bytes_accessed=10**6, transcendentals=0),
                name="filter_backward",
            )(grad_kernel, grid, ramp, rates, *nets, smalls, columns, sines, cosines)
            gs = gsmalls.T
            return (g1.T, gs[0], g2.T, gs[1], g3.T, gs[2], gs[3], gcols)

    else:
        feature_grid, ramp_unit = features(seq_len, feat_weight.shape[1])
        kernel, pull = jax.vjp(
            partial(filter_columns, feature_grid, ramp_unit, chan_start, chan, model),
            feat_weight[0],
            feat_bias[0],
            inner_weight[0],
            inner_bias[0],
            deep_weight[0],
            deep_bias[0],
            sine_freq[0],
            columns,
        )
        kern_spec = spectrum_of(kernel.reshape(chan, blocks, group).transpose(1, 0, 2), twist, table)

        def kernel_pull(grad_kernel):
            return pull(grad_kernel.transpose(1, 0, 2).reshape(chan, seq_len))

    mixed_chan, kept_spec = conv_forward(received, kern_spec, twist, table, skip_local)
    mixed = lax.all_to_all(mixed_chan, "seq", 0, 0, tiled=True).reshape(width, group)
    (y_cols,) = token_call(output_kernel, "output", common + [(mixed, True)], [flat_shape])

    middle_part = jnp.einsum("ct,oc->to", y_cols, full_out, preferred_element_type=F32)
    middle = residual + (scatter_rel(middle_part) + out_bias[0])
    normed_two, unit_two, scale_two = layer_norm(middle, norm2_gain[0], norm2_shift[0])
    rows_two = gather_rel(normed_two.astype(B16))

    grad_top = cotangent.astype(F32) * row_mask
    grad_mlp = grad_top.astype(B16)
    mlp_rows = gather_rel(grad_mlp)
    grad_act = jnp.dot(mlp_rows, full_down, preferred_element_type=F32)
    up_block = lax.dynamic_slice_in_dim(up_bias[0], rep * hidden, hidden, 0)
    pre_act = jnp.dot(rows_two, full_up, preferred_element_type=F32) + up_block
    phi = 0.5 * (1.0 + lax.erf(pre_act * math.sqrt(0.5)))
    act_rows = (pre_act * phi).astype(B16)
    slope = phi + pre_act * (jnp.exp(-0.5 * pre_act * pre_act) * (1.0 / math.sqrt(2.0 * math.pi)))
    grad_pre = (grad_act * slope).astype(B16)
    grad_two = scatter_rel(jnp.einsum("tf,df->td", grad_pre, full_up, preferred_element_type=F32))
    mlp_part = jnp.einsum("tf,of->to", act_rows, full_down, preferred_element_type=F32)
    layer_out = (middle + (scatter_rel(mlp_part) + down_bias[0])).astype(B16)
    term_down = jnp.einsum("to,tf->of", mlp_rows, act_rows, preferred_element_type=F32)
    term_up = jnp.einsum("td,tf->df", rows_two, grad_pre, preferred_element_type=F32)
    grad_two, term_down = lax.optimization_barrier((grad_two, term_down.astype(B16)))
    grad_down_bias = jnp.sum(grad_mlp.astype(F32), axis=0)
    grad_up_block = jnp.sum(grad_pre.astype(F32), axis=0)

    grad_down = lax.psum_scatter(
        term_down, "seq", scatter_dimension=0, tiled=True
    ).astype(F32)
    grad_up = ring_scatter(term_up.astype(B16))

    grad_unit_two, grad_gain_two, grad_shift_two = norm_back(
        grad_two, unit_two, scale_two, norm2_gain[0]
    )
    grad_middle = grad_top + grad_unit_two
    grad_mix = grad_middle.astype(B16)
    grad_out_bias = jnp.sum(grad_mix.astype(F32), axis=0)
    mix_rows = gather_rel(grad_mix)
    gy_cols = jnp.einsum("to,oc->ct", mix_rows, full_out, preferred_element_type=F32).astype(B16)
    term_out = jnp.einsum("to,ct->oc", mix_rows, y_cols, preferred_element_type=F32)
    grad_out = halve_scatter(term_out.astype(B16))

    grad_mixed, gate_first = token_call(
        grad_mix_kernel,
        "grad_mix",
        common + [(mixed, True), (gy_cols, True)],
        [flat_shape, jax.ShapeDtypeStruct((width, LANE), F32)],
    )
    gate_next = shift_seq(gate_first, -1)
    grads_chan = lax.all_to_all(grad_mixed.reshape(n_seq, chan, group), "seq", 0, 0, tiled=True)
    ggated_chan, grad_kernel = conv_backward(grads_chan, kept_spec, kern_spec, twist, table, skip_local)
    ggated = lax.all_to_all(ggated_chan, "seq", 0, 0, tiled=True).reshape(width, group)
    ggated_next = shift_seq(ggated[:, :LANE], -1)
    kernel_grads = kernel_pull(grad_kernel)
    grad_proj, col_sums = token_call(
        grad_proj_kernel,
        "grad_proj",
        common
        + [(mixed, True), (gy_cols, True), (ggated, True), (ggated_next, True), (gate_next, True)],
        [jax.ShapeDtypeStruct((3, width, group), B16), jax.ShapeDtypeStruct((width, 16), F32)],
    )

    one_part = jnp.einsum("pct,dpc->td", grad_proj, full_in, preferred_element_type=F32)
    grad_one = scatter_rel(one_part)
    term_in = jnp.einsum("td,pct->dpc", rows_one, grad_proj, preferred_element_type=F32)
    grad_in = halve_scatter(term_in.reshape(model, 3 * width).astype(B16))
    grad_in = grad_in.reshape(-1, 3, width)
    grad_unit_one, grad_gain_one, grad_shift_one = norm_back(
        grad_one, unit_one, scale_one, norm1_gain[0]
    )
    grad_tokens = grad_middle + grad_unit_one

    totals = [
        *kernel_grads[:7],
        grad_gain_one,
        grad_shift_one,
        grad_gain_two,
        grad_shift_two,
        grad_out_bias,
        grad_down_bias,
    ]
    packed = [rows128(t) for t in totals]
    group_part = jnp.concatenate([rows128(col_sums.T), rows128(grad_up_block)], axis=0)
    total, groups, owns = sync_small(jnp.concatenate(packed, axis=0), group_part, rows128(kernel_grads[7]))
    outs = []
    start = 0
    for t, p in zip(totals, packed):
        outs.append(total[start : start + p.shape[0]].reshape(-1)[: t.size].reshape((1,) + t.shape))
        start += p.shape[0]
    flat = groups.reshape(n_rep, -1)
    sums = flat[:, : 16 * width].reshape(n_rep, 16, width).transpose(1, 0, 2).reshape(16, model)
    grad_up_bias = flat[:, 16 * width : 16 * width + hidden].reshape(1, -1)
    filt = columns.shape[0]
    grad_kernel_weight = (
        owns.reshape(n_rep, n_seq, -1)[:, :, : filt * chan]
        .reshape(n_rep, n_seq, filt, chan)
        .transpose(2, 0, 1, 3)
        .reshape(1, filt, model)
    )
    pick = lambda offset: jnp.stack([sums[1 + 5 * p + offset] for p in range(3)])
    grad_skip = sums[0][None]
    grad_short_bias = pick(0)[None]
    grad_short_taps = jnp.stack([pick(3), pick(2), pick(1)])[None]
    grad_in_bias = pick(4)[None]
    return (
        layer_out,
        grad_tokens,
        grad_in[None],
        grad_in_bias,
        grad_short_taps,
        grad_short_bias,
        outs[0],
        outs[1],
        outs[2],
        outs[3],
        outs[4],
        outs[5],
        outs[6],
        grad_kernel_weight,
        grad_skip,
        grad_out[None],
        outs[11],
        outs[7],
        outs[8],
        outs[9],
        outs[10],
        grad_up[None],
        grad_up_bias,
        grad_down[None],
        outs[12],
    )


NN = ((1,), (0,))
NT = ((1,), (1,))
TN = ((0,), (0,))
PART = 64
REP, SEQ, AT, ITEM, OLDER, YOUNGER, OWNER, LEFT, RIGHT = 0, 1, 2, 3, 4, 5, 8, 16, 25
RING = [0, 2, 4, 6, 7, 5, 3, 1]
AHEAD = [(RING[i], RING[(i + 1) % 8]) for i in range(8)]
BACK = [(b, a) for a, b in AHEAD]


def meta_table(group):
    rows = []
    for seq in range(8):
        p = RING.index(seq)
        for rep in range(4):
            row = [rep, seq, (seq % 4) * group, seq // 4, int(seq % 4 != 0), int(seq % 4 != 3), 0, 0]
            row += [RING[(p + k) % 8] for k in (0, -1, 1, -2, 2, -3, 3, 4)]
            row += [RING[(p - k) % 8] for k in range(9)]
            row += [RING[(p + k) % 8] for k in range(9)]
            rows.append(row)
    return np.asarray(rows, np.int32)


COST = {"start": 4000, "setup": 4000, "filter_ahead": 6000}


def call(kernel, name, args, outs, scratch=(), limit=24, away=(), out_away=(), raw=()):
    away, out_away, raw = list(away), list(out_away), list(raw)
    hbm = pl.BlockSpec(memory_space=pltpu.HBM)

    def space(i, a):
        if i in away or i in raw:
            return hbm
        small = a.dtype == jnp.int32
        return pl.BlockSpec(memory_space=pltpu.SMEM if small else pltpu.VMEM)

    n_in, n_out, n_own = len(args), len(outs), len(scratch)
    bufs = [pltpu.VMEM(args[i].shape, args[i].dtype) for i in away]
    bufs += [pltpu.VMEM(outs[i].shape, outs[i].dtype) for i in out_away]
    sems = [pltpu.SemaphoreType.DMA((len(bufs),))] if bufs else []

    def body(*refs):
        ins, results = list(refs[:n_in]), list(refs[n_in : n_in + n_out])
        own, mine = refs[n_in + n_out : n_in + n_out + n_own], refs[n_in + n_out + n_own :]
        copies = []
        for k, i in enumerate(away):
            copies.append(pltpu.make_async_copy(ins[i], mine[k], mine[-1].at[k]))
            ins[i] = mine[k]
        for copy in copies:
            copy.start()
        for copy in copies:
            copy.wait()
        copies = []
        for k, i in enumerate(out_away, len(away)):
            copies.append(pltpu.make_async_copy(mine[k], results[i], mine[-1].at[k]))
            results[i] = mine[k]
        kernel(*ins, *results, *own)
        for copy in copies:
            copy.start()
        for copy in copies:
            copy.wait()

    return pl.pallas_call(
        body,
        out_shape=outs,
        in_specs=[space(i, a) for i, a in enumerate(args)],
        out_specs=[hbm if i in out_away or (-1 - i) in raw else pl.BlockSpec(memory_space=pltpu.VMEM) for i in range(n_out)],
        scratch_shapes=list(scratch) + bufs + sems,
        compiler_params=pltpu.CompilerParams(vmem_limit_bytes=limit * 2**20),
        cost_estimate=pl.CostEstimate(flops=COST.get(name, 1) * 10**6, bytes_accessed=10**5, transcendentals=0),
        name=name,
    )(*args)


def shape(dims, kind):
    return jax.ShapeDtypeStruct(tuple(dims), kind)


def dot(left, right, dims):
    return lax.dot_general(left, right, (dims, ((), ())), preferred_element_type=F32)


def place(index):
    return pl.ds(pl.multiple_of(index * LANE, LANE), LANE)


def normed_of(rows):
    centred = rows - jnp.mean(rows, axis=1, keepdims=True)
    inverse = lax.rsqrt(jnp.mean(centred * centred, axis=1, keepdims=True) + EPS)
    return centred * inverse, inverse


def item_length(meta_ref, len_ref):
    return jnp.where(meta_ref[ITEM] == 0, len_ref[0], len_ref[1])


def lane_masks(meta_ref, len_ref, size):
    lane = lax.broadcasted_iota(jnp.int32, (1, size), 1)
    real = (meta_ref[AT] - LANE + lane < item_length(meta_ref, len_ref)).astype(F32)
    older, younger = meta_ref[OLDER].astype(F32), meta_ref[YOUNGER].astype(F32)
    exists = jnp.where(lane < LANE, older, jnp.where(lane >= size - LANE, younger, 1.0))
    return real, exists


def start_kernel(x_ref, gain_ref, shift_ref, in_ref, out_w_ref, out_ref, io_ref):
    width = out_w_ref.shape[2]
    for p in range(3):
        io_ref[:, p * width : (p + 1) * width] = in_ref[p]
    io_ref[:, 3 * width :] = out_w_ref[0]
    unit, _ = normed_of(x_ref[...].astype(F32))
    out_ref[...] = (unit * gain_ref[...] + shift_ref[...]).astype(B16)


def halves_kernel(left_ref, right_ref, a_ref, b_ref):
    half = a_ref.shape[0]
    a_ref[...] = left_ref[:half]
    b_ref[...] = right_ref[half:]


def assemble_kernel(meta_ref, p0, p1, p2, p3, p4, p5, p6, a_ref, b_ref, out_ref):
    for k, ref in enumerate((p0, p1, p2, p3, p4, p5, p6)):
        out_ref[meta_ref[OWNER + k]] = ref[...]
    half = a_ref.shape[0]
    out_ref[meta_ref[OWNER + 7], :half] = a_ref[...]
    out_ref[meta_ref[OWNER + 7], half:] = b_ref[...]


def own_mask(meta_ref, len_ref, rows):
    row = lax.broadcasted_iota(jnp.int32, (rows, 1), 0)
    return (meta_ref[AT] + meta_ref[REP] * rows + row < item_length(meta_ref, len_ref)).astype(F32)


def setup_kernel(
    meta_ref, len_ref, top_ref, up_ref, down_ref, taps_ref, short_bias_ref, in_bias_ref, up_bias_ref, skip_ref, rate_ref,
    kern_w_ref, feat_ref, fb_ref, ib_ref, db_ref, sf_ref,
    rows_ref, ud_ref, cols_ref, upb_ref, chan_ref, columns_ref, small_col_ref, small_row_ref, w1_ref, *rest
):
    sems = rest[-1]
    copies = [
        pltpu.make_async_copy(up_ref, ud_ref.at[pl.ds(0, 1)], sems.at[0]),
        pltpu.make_async_copy(down_ref, ud_ref.at[pl.ds(1, 1)], sems.at[1]),
    ]
    for copy in copies:
        copy.start()
    top, taps, short_bias, in_bias, up_bias, skip, rate, kern_w, feat, fb, ib, db, sf = (
        top_ref, taps_ref, short_bias_ref, in_bias_ref, up_bias_ref, skip_ref, rate_ref, kern_w_ref, feat_ref,
        fb_ref, ib_ref, db_ref, sf_ref,
    )
    mask = own_mask(meta_ref, len_ref, top.shape[0])
    rows_ref[...] = (top[...].astype(F32) * mask).astype(B16)
    width = cols_ref.shape[0]
    chan = chan_ref.shape[0]
    rep, seq = meta_ref[REP], meta_ref[SEQ]
    lanes = pl.ds(pl.multiple_of(rep * width, width), width)
    rows = [taps[j, p, :, lanes] for j in range(3) for p in range(3)]
    rows += [short_bias[p, :, lanes] for p in range(3)] + [in_bias[p, :, lanes] for p in range(3)]
    stack = jnp.concatenate(rows + [jnp.zeros((LANE - 15, width), F32)], axis=0)
    cols_ref[...] = stack.T[:, :16]
    upb_ref[...] = up_bias[:, pl.ds(pl.multiple_of(rep * upb_ref.shape[1], LANE), upb_ref.shape[1])]
    turn = width - seq * chan
    stack = jnp.concatenate([skip[:, lanes], rate[:, lanes], jnp.zeros((LANE - 2, width), F32)], axis=0)
    chan_ref[...] = pltpu.roll(stack, turn, 1)[:, :LANE].T[:chan, :2]
    columns_ref[...] = pltpu.roll(kern_w[0, :, lanes], turn, 1)[:, :chan]
    filt = small_row_ref.shape[1]
    small = jnp.concatenate([fb[...], ib[...], db[...], sf[...]], axis=0)
    small_row_ref[...] = small
    wide = jnp.concatenate([small, jnp.zeros((4, LANE - filt), F32)], axis=1)
    wide = jnp.concatenate([wide, jnp.zeros((LANE - 4, LANE), F32)], axis=0)
    small_col_ref[...] = wide.T[:filt, :4]
    w1_ref[...] = jnp.concatenate([feat[i] for i in range(feat.shape[0])], axis=0)
    for copy in copies:
        copy.wait()


def edges_kernel(meta_ref, x0, x1, x2, x3, last_ref, first_ref):
    rep = meta_ref[REP]
    refs = (x0, x1, x2, x3)

    def chosen(index, lo):
        value = refs[0][lo : lo + HALO]
        for i in range(1, 4):
            value = jnp.where(index == i, refs[i][lo : lo + HALO].astype(F32), value.astype(F32))
        return value.astype(B16)

    last_ref[...] = chosen(rep ^ 3, x0.shape[0] - HALO)
    first_ref[...] = chosen(rep, 0)


def ext_of(proj_ref, halo_ref, exists, p, rows):
    return (
        jnp.concatenate(
            [halo_ref[p, rows, :LANE], proj_ref[p, rows, :], halo_ref[p, rows, LANE:]], axis=1
        ).astype(F32)
        * exists
    )


def short_from(ext, cols, p):
    return (
        cols[:, p : p + 1] * pltpu.roll(ext, 2, 1)
        + cols[:, 3 + p : 4 + p] * pltpu.roll(ext, 1, 1)
        + cols[:, 6 + p : 7 + p] * ext
        + cols[:, 9 + p : 10 + p]
    )


def project_kernel(
    meta_ref, len_ref, x0, x1, x2, x3, before_ref, after_ref, cols_ref,
    p0, p1, p2, p3, p4, p5, p6, a_ref, b_ref, io_full_ref, proj_ref, halo_ref, gated_ref
):
    assemble_kernel(meta_ref, p0, p1, p2, p3, p4, p5, p6, a_ref, b_ref, io_full_ref)
    io_ref = io_full_ref.reshape(-1, io_full_ref.shape[2])
    rep = meta_ref[REP]
    width, group = gated_ref.shape
    weight = io_ref[:, : 3 * width]
    for i, x_ref in enumerate((x0, x1, x2, x3)):
        cut = dot(x_ref[...], weight, NN).T
        for p in range(3):
            proj_ref[p, :, place(rep ^ i)] = (
                cut[p * width : (p + 1) * width] + cols_ref[:, 12 + p : 13 + p]
            ).astype(B16)
    edge = dot(jnp.concatenate([before_ref[...], after_ref[...]], axis=0), weight, NN)
    gap = jnp.zeros((LANE - HALO, 3 * width), F32)
    edge = jnp.concatenate([gap, edge, gap], axis=0).T
    for p in range(3):
        halo_ref[p] = (edge[p * width : (p + 1) * width] + cols_ref[:, 12 + p : 13 + p]).astype(B16)
    mask, exists = lane_masks(meta_ref, len_ref, group + 2 * LANE)
    for lo in range(0, width, PART):
        rows = slice(lo, lo + PART)
        cols = cols_ref[rows, :]
        gate_in = short_from(ext_of(proj_ref, halo_ref, exists, 1, rows), cols, 1)
        values = short_from(ext_of(proj_ref, halo_ref, exists, 2, rows), cols, 2)
        gated_ref[rows, :] = (values * gate_in * mask)[:, LANE:-LANE].astype(B16)


def out_project_kernel(
    meta_ref, len_ref, proj_ref, halo_ref, cols_ref, io_ref, mixed_ref, y_ref, give3_ref, give1_ref, keep2_ref, keep0_ref
):
    rep = meta_ref[REP]
    width, group = mixed_ref.shape
    _, exists = lane_masks(meta_ref, len_ref, group + 2 * LANE)
    for lo in range(0, width, LANE):
        rows = slice(lo, lo + LANE)
        gate_out = short_from(ext_of(proj_ref, halo_ref, exists, 0, rows), cols_ref[rows, :], 0)
        y = gate_out[:, LANE:-LANE] * mixed_ref[rows, :].astype(F32)
        for j in range(4):
            y_ref[rep ^ j, :, rows] = y[:, j * LANE : (j + 1) * LANE].T.astype(B16)
    outs = (keep0_ref, give1_ref, keep2_ref, give3_ref)
    left = y_ref[...].reshape(-1, width)
    rows = y_ref.shape[1]
    for lo in range(0, io_ref.shape[0], 256):
        part = dot(left, io_ref[lo : lo + 256, 3 * width :], NT)
        for i, ref in enumerate(outs):
            ref[:, lo : lo + 256] = part[i * rows : (i + 1) * rows].astype(ref.dtype)


def halves_far_kernel(left_ref, right_ref, a_ref, b_ref, sems):
    half = a_ref.shape[0]
    copies = [
        pltpu.make_async_copy(left_ref.at[pl.ds(0, half)], a_ref, sems.at[0]),
        pltpu.make_async_copy(right_ref.at[pl.ds(half, half)], b_ref, sems.at[1]),
    ]
    for copy in copies:
        copy.start()
    for copy in copies:
        copy.wait()


def assemble_far_kernel(meta_ref, p0, p1, p2, p3, p4, p5, p6, a_ref, b_ref, out_ref, sems):
    half = a_ref.shape[0]
    last = out_ref.at[meta_ref[OWNER + 7]]
    copies = [
        pltpu.make_async_copy(ref, out_ref.at[meta_ref[OWNER + k]], sems.at[k])
        for k, ref in enumerate((p0, p1, p2, p3, p4, p5, p6))
    ]
    copies.append(pltpu.make_async_copy(a_ref, last.at[pl.ds(0, half)], sems.at[7]))
    copies.append(pltpu.make_async_copy(b_ref, last.at[pl.ds(half, half)], sems.at[8]))
    for copy in copies:
        copy.start()
    for copy in copies:
        copy.wait()


def norm_second_kernel(x_ref, keep_ref, near_ref, far_ref, bias_ref, gain_ref, shift_ref, middle_ref, out_ref):
    middle = x_ref[...].astype(F32) + (
        keep_ref[...] + near_ref[...].astype(F32) + far_ref[...].astype(F32) + bias_ref[...]
    )
    middle_ref[...] = middle
    unit, _ = normed_of(middle)
    out_ref[...] = (unit * gain_ref[...] + shift_ref[...]).astype(B16)


def mlp_kernel(x0, x1, x2, x3, g0, g1, g2, g3, ud_ref, bias_ref, act_ref, gpre_ref, sum_ref):
    step = 256
    rows, model = x0.shape
    pieces = ((x0, g0), (x1, g1), (x2, g2), (x3, g3))
    for lo in range(0, act_ref.shape[1], step):
        cut = slice(lo, lo + step)
        up = ud_ref[:, 0, :, cut].reshape(model, step)
        down = ud_ref[:, 1, :, cut].reshape(model, step)
        total = None
        for i, (x_ref, g_ref) in enumerate(pieces):
            at = slice(i * rows, (i + 1) * rows)
            pre = dot(x_ref[...], up, NN) + bias_ref[:, cut]
            gact = dot(g_ref[...], down, NN)
            phi = 0.5 * (1.0 + lax.erf(pre * math.sqrt(0.5)))
            slope = phi + pre * (jnp.exp(-0.5 * pre * pre) * (1.0 / math.sqrt(2.0 * math.pi)))
            act_ref[at, cut] = (pre * phi).astype(B16)
            gpre = (gact * slope).astype(B16)
            gpre_ref[at, cut] = gpre
            part = jnp.sum(gpre.astype(F32), axis=0, keepdims=True)
            total = part if total is None else total + part
        sum_ref[:, cut] = total


def rows_kernel(which, left_ref, ud_ref, give3_ref, give1_ref, keep2_ref, keep0_ref):
    rows, model = give3_ref.shape
    owned = ud_ref.shape[2]
    outs = (keep0_ref, give1_ref, keep2_ref, give3_ref)
    for k in range(0, ud_ref.shape[0], 2):
        weight = ud_ref[k : k + 2, which].reshape(2 * owned, -1)
        part = dot(left_ref[...], weight, NT)
        for i, ref in enumerate(outs):
            ref[:, k * owned : (k + 2) * owned] = part[i * rows : (i + 1) * rows].astype(ref.dtype)


def mlp_grad_kernel(meta_ref, x0, x1, x2, x3, g0, g1, g2, g3, act_ref, gpre_ref, out_ref, a_ref, b_ref):
    grad_pair((x0, x1, x2, x3), gpre_ref[...], out_ref, slice(None), 0)
    grad_pair((g0, g1, g2, g3), act_ref[...], out_ref, slice(None), out_ref.shape[3] // 2)
    give_first(meta_ref, out_ref, a_ref, b_ref)


def norm_second_back_kernel(
    meta_ref, len_ref, keep_ref, near_ref, far_ref, middle_ref, top_ref, gain_ref, out_ref, gx_ref, sum_ref
):
    grad = keep_ref[...] + near_ref[...].astype(F32) + far_ref[...].astype(F32)
    unit, inverse = normed_of(middle_ref[...])
    scaled = grad * gain_ref[...]
    one = jnp.mean(scaled, axis=1, keepdims=True)
    two = jnp.mean(scaled * unit, axis=1, keepdims=True)
    top = top_ref[...].astype(F32) * own_mask(meta_ref, len_ref, top_ref.shape[0])
    out = top + inverse * (scaled - one - unit * two)
    out_ref[...] = out
    gx = out.astype(B16)
    gx_ref[...] = gx
    rows = [grad * unit, grad, gx.astype(F32), top]
    sums = [jnp.sum(r, axis=0, keepdims=True) for r in rows]
    sum_ref[...] = jnp.concatenate(sums + [jnp.zeros((4, sums[0].shape[1]), F32)], axis=0)


def grad_gate_kernel(
    meta_ref, len_ref, x0, x1, x2, x3, io_ref, proj_ref, halo_ref, cols_ref, mixed_ref, gy_ref, first_ref, gmix_ref
):
    rep = meta_ref[REP]
    width, group = mixed_ref.shape
    _, exists = lane_masks(meta_ref, len_ref, group + 2 * LANE)
    weight = io_ref[:, 3 * width :]
    for i, x_ref in enumerate((x0, x1, x2, x3)):
        gy_ref[:, place(rep ^ i)] = dot(x_ref[...], weight, NN).T.astype(B16)
    for lo in range(0, width, PART):
        rows = slice(lo, lo + PART)
        gate_out = short_from(ext_of(proj_ref, halo_ref, exists, 0, rows), cols_ref[rows, :], 0)
        gy = gy_ref[rows, :].astype(F32)
        gmix_ref[rows, :] = (gy * gate_out[:, LANE:-LANE]).astype(B16)
        first_ref[rows, :] = gy[:, :LANE] * mixed_ref[rows, :LANE].astype(F32)


def conv_back_kernel(
    spec_ref, kern_ref, twist_ref, hi_ref, lo_ref, chan_ref, g_ref, out_ref, grad_kern_ref, z_ref, p_ref
):
    blocks, rows, length = twist_ref.shape[0], g_ref.shape[1], g_ref.shape[2]
    short_blocks = blocks // 4
    span = blocks * rows
    first = [g_ref[b].astype(F32) for b in range(blocks)]
    second = [g_ref[blocks + b].astype(F32) for b in range(short_blocks)]
    turn_rows(first, twist_ref, z_ref, 0, blocks)
    turn_rows(second, twist_ref, z_ref, span, blocks)
    grad = dot_split(z_ref[...], hi_ref[...], lo_ref[...], ((1,), (0,)))
    kern = kern_ref[...]
    p_ref[0:span] = times(grad[:span], kern, True)
    p_ref[span : 2 * span] = times(grad[span:], kern, True)
    p_ref[2 * span :] = times(grad[:span], spec_ref[0:span], True) + times(grad[span:], spec_ref[span:], True)
    w = dot_split(p_ref[...], hi_ref[...], lo_ref[...], ((1,), (1,)))
    skip = chan_ref[:, 0:1]
    for b in range(blocks):
        acc = (back_rows(w, 0, rows, b, twist_ref, blocks) + skip * first[b]).astype(B16)
        out_ref[b] = acc
        if b < short_blocks:
            acc = (back_rows(w, span, rows, b, twist_ref, blocks) + skip * second[b]).astype(B16)
        else:
            acc = jnp.zeros((rows, length), B16)
        out_ref[blocks + b] = acc
        grad_kern_ref[b] = back_rows(w, 2 * span, rows, b, twist_ref, blocks)


def conv_ahead_kernel(kern_ref, twist_ref, hi_ref, lo_ref, chan_ref, x_ref, out_ref, spec_ref, z_ref):
    conv_forward_kernel(
        twist_ref.shape[0] // 4, x_ref, kern_ref, twist_ref, hi_ref, lo_ref, chan_ref.at[:, 0:1], out_ref, spec_ref, z_ref
    )


def filter_ahead_kernel(
    chan_ref, w1_ref, small_ref, columns_ref, grid_ref, ramp_ref, w2_ref, w3_ref, twist_ref, hi_ref, lo_ref,
    spec_ref, sin_ref, cos_ref, z_ref
):
    filter_forward_kernel(
        grid_ref, ramp_ref, chan_ref.at[:, 1:2], w1_ref, w2_ref.at[0], w3_ref.at[0], small_ref, columns_ref,
        twist_ref, hi_ref, lo_ref, spec_ref, sin_ref, cos_ref, z_ref
    )


def halves_of(values):
    top = values.astype(B16)
    return top, (values - top.astype(F32)).astype(B16)


def dot_halves(left, right, dims):
    return dot(left[0], right[0], dims) + dot(left[1], right[0], dims) + dot(left[0], right[1], dims)


def filter_back_kernel(
    meta_ref, gk_ref, grid_ref, ramp_ref, chan_ref, w1_ref, w2_ref, w3_ref, col_ref, row_ref, columns_ref, sin_ref, cos_ref,
    side_ref, wide_ref
):
    freq, freq_row = col_ref[:, 3:4], row_ref[3:4, :]
    filt = freq.shape[0]
    gk = jnp.concatenate([gk_ref[b] for b in range(gk_ref.shape[0])], axis=1)
    gk = halves_of(gk * jnp.exp(-chan_ref[:, 1:2] * ramp_ref[...]))
    gcols = dot_halves(halves_of(sin_ref[2]), gk, NT)
    chan, width = gcols.shape[1], wide_ref.shape[1]
    row = lax.broadcasted_iota(jnp.int32, (chan, width), 0)
    lane = lax.broadcasted_iota(jnp.int32, (chan, width), 1)
    pick = (lane == row + meta_ref[SEQ] * chan).astype(F32)
    wide_ref[...] = dot_high(gcols, pick, NN)
    grad = dot_halves(halves_of(columns_ref[...]), gk, NN)
    ones = jnp.ones((16, grad.shape[1]), B16)
    gfreq = jnp.zeros((1, filt), F32)
    grads, biases = [None] * 3, [None] * 3
    for i, weight in ((2, w3_ref[0]), (1, w2_ref[0]), (0, w1_ref[...])):
        turn = grad * cos_ref[i]
        pair = halves_of(turn)
        below = halves_of(sin_ref[i - 1] if i else grid_ref[...])
        raw = dot_halves(below, pair, NT)
        total = (dot(ones, pair[0], NT) + dot(ones, pair[1], NT))[0:1]
        grads[i] = raw * freq_row
        biases[i] = total * freq_row
        gfreq = gfreq + jnp.sum(raw * weight, axis=0, keepdims=True) + total * row_ref[i : i + 1, :]
        if i:
            grad = dot_halves(halves_of(weight * freq_row), pair, NN)
    gap = jnp.zeros((filt - grads[0].shape[0], filt), F32)
    small = jnp.concatenate(biases + [gfreq, jnp.zeros((filt - 4, filt), F32)], axis=0)
    side_ref[...] = jnp.concatenate(
        [grads[1], grads[2], jnp.concatenate([grads[0], gap], axis=0), small], axis=1
    )


def summed(value):
    total = value[:, :LANE]
    for k in range(LANE, value.shape[1], LANE):
        total = total + value[:, k : k + LANE]
    return jnp.sum(total, axis=1, keepdims=True)


def short_back(ext, cols, gshort, p, mid):
    size = ext.shape[1]
    mine = gshort[:, mid]
    gproj = (
        cols[:, 6 + p : 7 + p] * gshort
        + cols[:, 3 + p : 4 + p] * pltpu.roll(gshort, size - 1, 1)
        + cols[:, p : p + 1] * pltpu.roll(gshort, size - 2, 1)
    )[:, mid].astype(B16).astype(F32)
    sums = [
        summed(mine),
        summed(mine * ext[:, mid]),
        summed(mine * pltpu.roll(ext, 1, 1)[:, mid]),
        summed(mine * pltpu.roll(ext, 2, 1)[:, mid]),
        summed(gproj),
    ]
    return gproj, sums


def grad_first_kernel(
    meta_ref, len_ref, proj_ref, halo_ref, cols_ref, mixed_ref, gy_ref, onext_ref, io_ref, tok_ref, sum_ref, part_ref
):
    rep = meta_ref[REP]
    width, group = mixed_ref.shape
    size = group + 2 * LANE
    mask, exists = lane_masks(meta_ref, len_ref, size)
    mid = slice(LANE, size - LANE)
    next_on = exists[:, size - LANE :]
    columns = []
    for lo in range(0, width, PART):
        rows = slice(lo, lo + PART)
        cols = cols_ref[rows, :]
        gy = gy_ref[rows, :].astype(F32)
        gout = gy * mixed_ref[rows, :].astype(F32)
        gshort = jnp.concatenate([jnp.zeros((PART, LANE), F32), gout, onext_ref[rows, :] * next_on], axis=1)
        gproj, sums = short_back(ext_of(proj_ref, halo_ref, exists, 0, rows), cols, gshort, 0, mid)
        for j in range(4):
            tok_ref[rep ^ j, :, rows] = gproj[:, j * LANE : (j + 1) * LANE].T.astype(B16)
        columns.append(jnp.concatenate(sums + [jnp.zeros((PART, LANE - 5), F32)], axis=1))
    sum_ref[...] = jnp.concatenate(columns, axis=0).T[:8]
    part_ref[...] = dot(tok_ref[...].reshape(-1, width), io_ref[:, :width], NT)


def grad_short_kernel(
    meta_ref, len_ref, proj_ref, halo_ref, cols_ref, gy_ref, io_ref, before_ref,
    x0, x1, x2, x3, gain_ref, shift_ref, ggated_ref, gnext_ref,
    tok_ref, sum_ref, norm_ref, give3_ref, give1_ref, keep2_ref, keep0_ref
):
    rep = meta_ref[REP]
    width, group = gy_ref.shape
    size = group + 2 * LANE
    mask, exists = lane_masks(meta_ref, len_ref, size)
    mid = slice(LANE, size - LANE)
    columns = []
    for lo in range(0, width, PART):
        rows = slice(lo, lo + PART)
        cols = cols_ref[rows, :]
        ext = [ext_of(proj_ref, halo_ref, exists, p, rows) for p in (1, 2)]
        short = [short_from(ext[p - 1], cols, p) for p in (1, 2)]
        ggated = (
            jnp.concatenate(
                [jnp.zeros((PART, LANE), F32), ggated_ref[rows, :].astype(F32), gnext_ref[rows, :].astype(F32)], axis=1
            )
            * mask
            * exists
        )
        gate_out = short_from(ext_of(proj_ref, halo_ref, exists, 0, rows), cols, 0)[:, mid]
        gated = short[1][:, mid] * short[0][:, mid] * mask[:, mid]
        sums = [summed(gy_ref[rows, :].astype(F32) * gate_out * gated)]
        for p in (1, 2):
            gproj, more = short_back(ext[p - 1], cols, ggated * short[2 - p], p, mid)
            sums += more
            at = slice((p - 1) * width + lo, (p - 1) * width + lo + PART)
            for j in range(4):
                tok_ref[rep ^ j, :, at] = gproj[:, j * LANE : (j + 1) * LANE].T.astype(B16)
        columns.append(jnp.concatenate(sums + [jnp.zeros((PART, LANE - 11), F32)], axis=1))
    sum_ref[...] = jnp.concatenate(columns, axis=0).T[:16]
    outs = (keep0_ref, give1_ref, keep2_ref, give3_ref)
    left = tok_ref[...].reshape(-1, 2 * width)
    tall = tok_ref.shape[1]
    for lo in range(0, io_ref.shape[0], 256):
        cut = slice(lo, lo + 256)
        part = dot(left, io_ref[cut, width : 3 * width], NT) + before_ref[:, cut]
        plain = jnp.sum(part, axis=0, keepdims=True)
        cross = None
        for i, (ref, x_ref) in enumerate(zip(outs, (x0, x1, x2, x3))):
            mine = part[i * tall : (i + 1) * tall]
            ref[:, cut] = mine.astype(ref.dtype)
            two = jnp.sum(mine * x_ref[:, cut].astype(F32), axis=0, keepdims=True)
            cross = two if cross is None else cross + two
        norm_ref[0:1, cut] = (cross - shift_ref[:, cut] * plain) / gain_ref[:, cut]
        norm_ref[1:2, cut] = plain


def give_first(meta_ref, term_ref, a_ref, b_ref):
    half = a_ref.shape[2]
    seq = meta_ref[SEQ]
    s0, s1 = seq & 1, (seq >> 1) & 1
    for i in range(2):
        for j in range(2):
            a_ref[i, j] = term_ref[i, j, 1 - s0, :half]
            b_ref[i, j] = term_ref[i, 1 - s1, j, half:]


def grad_pair(refs, right, out_ref, lanes, base=0):
    owned = refs[0].shape[1] // 8
    for k in range(0, 8, 2):
        left = jnp.concatenate([r[:, k * owned : (k + 2) * owned] for r in refs], axis=0)
        part = dot(left, right, TN).astype(B16)
        out_ref[k // 4, (k // 2) % 2, 0, base : base + owned, lanes] = part[:owned]
        out_ref[k // 4, (k // 2) % 2, 1, base : base + owned, lanes] = part[owned:]


def grad_early_kernel(meta_ref, g0, g1, g2, g3, y_ref, x0, x1, x2, x3, tok_ref, out_ref, a_ref, b_ref):
    width = y_ref.shape[2]
    grad_pair((g0, g1, g2, g3), y_ref[...].reshape(-1, width), out_ref, slice(0, width))
    grad_pair((x0, x1, x2, x3), tok_ref[...].reshape(-1, width), out_ref, slice(width, 2 * width))
    give_first(meta_ref, out_ref, a_ref, b_ref)


def grad_late_kernel(meta_ref, x0, x1, x2, x3, tok_ref, out_ref, a_ref, b_ref):
    width = tok_ref.shape[2]
    grad_pair((x0, x1, x2, x3), tok_ref[...].reshape(-1, width), out_ref, slice(0, width))
    give_first(meta_ref, out_ref, a_ref, b_ref)


def halve_one_kernel(meta_ref, term_ref, a_in, b_in, keep_a, keep_b, give_a, give_b):
    half = a_in.shape[2]
    seq = meta_ref[SEQ]
    s0, s1 = seq & 1, (seq >> 1) & 1
    for i in range(2):
        keep_a[i] = term_ref[i, s1, s0, :half].astype(F32) + a_in[i, s1].astype(F32)
        give_a[i] = (term_ref[i, 1 - s1, s0, :half].astype(F32) + a_in[i, 1 - s1].astype(F32)).astype(B16)
        keep_b[i] = term_ref[i, s1, s0, half:].astype(F32) + b_in[i, s0].astype(F32)
        give_b[i] = (term_ref[i, s1, 1 - s0, half:].astype(F32) + b_in[i, 1 - s0].astype(F32)).astype(B16)


def halve_two_kernel(meta_ref, keep_a_in, keep_b_in, a_in, b_in, keep_a, keep_b, give_a, give_b):
    s2 = meta_ref[SEQ] >> 2
    keep_a[...] = keep_a_in[s2] + a_in[s2].astype(F32)
    give_a[...] = (keep_a_in[1 - s2] + a_in[1 - s2].astype(F32)).astype(B16)
    keep_b[...] = keep_b_in[s2] + b_in[s2].astype(F32)
    give_b[...] = (keep_b_in[1 - s2] + b_in[1 - s2].astype(F32)).astype(B16)


def add_last_kernel(keep_ref, came_ref, out_ref):
    out_ref[0] = keep_ref[...] + came_ref[...].astype(F32)


def early_last_kernel(keep_a, keep_b, a_in, b_in, out_ref, in_ref):
    half, width = keep_a.shape[0], out_ref.shape[2]
    for keep, came, rows in ((keep_a, a_in, slice(0, half)), (keep_b, b_in, slice(half, 2 * half))):
        out_ref[0, rows] = keep[:, :width] + came[:, :width].astype(F32)
        in_ref[rows] = keep[:, width:] + came[:, width:].astype(F32)


def late_last_kernel(keep_a, keep_b, a_in, b_in, first_ref, out_ref):
    half, width = keep_a.shape[0], out_ref.shape[3]
    out_ref[0, 0] = first_ref[...]
    for keep, came, rows in ((keep_a, a_in, slice(0, half)), (keep_b, b_in, slice(half, 2 * half))):
        for p in range(2):
            lanes = slice(p * width, (p + 1) * width)
            out_ref[0, 1 + p, rows] = keep[:, lanes] + came[:, lanes].astype(F32)


def norm_first_back_kernel(keep_ref, near_ref, far_ref, x_ref, middle_ref, gain_ref, out_ref):
    grad = keep_ref[...] + near_ref[...].astype(F32) + far_ref[...].astype(F32)
    unit, inverse = normed_of(x_ref[...].astype(F32))
    scaled = grad * gain_ref[...]
    one = jnp.mean(scaled, axis=1, keepdims=True)
    two = jnp.mean(scaled * unit, axis=1, keepdims=True)
    out_ref[...] = middle_ref[...] + inverse * (scaled - one - unit * two)


def layer_out_kernel(keep_ref, near_ref, far_ref, middle_ref, bias_ref, out_ref):
    part = keep_ref[...] + near_ref[...].astype(F32) + far_ref[...].astype(F32)
    out_ref[...] = (middle_ref[...] + (part + bias_ref[...])).astype(B16)


def heads_kernel(in_ref, out_ref):
    out_ref[...] = in_ref[:, :LANE]


def add_far_kernel(keep_ref, came_ref, out_ref):
    out_ref[...] = (keep_ref[...] + came_ref[...].astype(F32)).astype(B16)


HALF = 88


def pack_small_kernel(side_ref, wide_ref, col0_ref, col_ref, up_ref, one_ref, two_ref, out_ref):
    filt, width = side_ref.shape
    out_ref[:filt] = side_ref[...]
    at = filt
    for ref, count in ((one_ref, 2), (two_ref, 4)):
        for r in range(count):
            for k in range(4):
                out_ref[at : at + 1] = ref[r : r + 1, k * width : (k + 1) * width]
                at += 1
    out_ref[HALF : HALF + 1] = col_ref[0:1]
    out_ref[HALF + 1 : HALF + 6] = col0_ref[0:5]
    out_ref[HALF + 6 : HALF + 16] = col_ref[1:11]
    for k in range(4):
        out_ref[HALF + 16 + k : HALF + 17 + k] = up_ref[:, k * width : (k + 1) * width]
    out_ref[HALF + 20 : HALF + 24] = jnp.zeros((4, width), F32)
    out_ref[HALF + 24 :] = wide_ref[...]


def add_small_kernel(mine_ref, came_ref, out_ref):
    out_ref[...] = mine_ref[...] + came_ref[...]


def list_small_kernel(meta_ref, mine_ref, came_ref, out_ref):
    y = meta_ref[REP] >> 1
    out_ref[:HALF] = mine_ref[:HALF] + came_ref[:HALF]
    out_ref[pl.ds(pl.multiple_of((1 + y) * HALF, 8), HALF)] = mine_ref[HALF:]
    out_ref[pl.ds(pl.multiple_of((2 - y) * HALF, 8), HALF)] = came_ref[HALF:]


def unpack_small_kernel(
    meta_ref, mine_ref, came_ref,
    in_bias, taps, short_bias, fw, fb, iw, ib, dw, db, sf, kern_w, skip, out_b, n1g, n1s, n2g, n2s, up_b, down_b
):
    core = meta_ref[REP] & 1
    filt, width = iw.shape[2], mine_ref.shape[1]
    total = mine_ref[:HALF] + came_ref[:HALF]
    iw[0] = total[:filt, :filt]
    dw[0] = total[:filt, filt : 2 * filt]
    for k in range(fw.shape[0]):
        fw[k] = total[k : k + 1, 2 * filt : 3 * filt]
    for k, ref in enumerate((fb, ib, db, sf)):
        ref[...] = total[k : k + 1, 3 * filt :]
    at = filt
    for ref in (n1g, n1s, n2g, n2s, out_b, down_b):
        for k in range(4):
            ref[:, k * width : (k + 1) * width] = total[at : at + 1]
            at += 1
    for y in range(2):
        lo = (1 + y) * HALF
        mine, came = mine_ref[lo : lo + HALF], came_ref[lo : lo + HALF]
        for c in range(2):
            block = jnp.where(core == c, mine, came)
            lanes = slice((2 * y + c) * width, (2 * y + c + 1) * width)
            skip[:, lanes] = block[0:1]
            for p in range(3):
                row = 1 + 5 * p
                short_bias[p, :, lanes] = block[row : row + 1]
                for j in range(3):
                    taps[j, p, :, lanes] = block[row + 3 - j : row + 4 - j]
                in_bias[p, :, lanes] = block[row + 4 : row + 5]
            for k in range(4):
                lo_up = (2 * y + c) * 4 * width + k * width
                up_b[:, lo_up : lo_up + width] = block[16 + k : 17 + k]
            kern_w[0, :, lanes] = block[24 : 24 + filt]


def tie(values, *others):
    return lax.optimization_barrier((values, others))[0]


class RingGather:
    def __init__(self, name, meta, shard, far=False):
        self.name, self.meta, self.far = name, meta, far
        self.pieces = [shard]
        self.send(shard, shard)

    def send(self, left, right):
        self.came = (lax.ppermute(left, "seq", AHEAD), lax.ppermute(right, "seq", BACK))

    def step(self, *others):
        left, right = tie(self.came, *others)
        self.pieces += [left, right]
        count = len(self.pieces)
        if count == 7:
            half = shape((left.shape[0] // 2,) + left.shape[1:], B16)
            if self.far:
                left, right = call(
                    halves_far_kernel, self.name + "_halves", [left, right], [half, half],
                    scratch=[pltpu.SemaphoreType.DMA((2,))], raw=[0, 1, -1, -2],
                )
            else:
                left, right = call(halves_kernel, self.name + "_halves", [left, right], [half, half])
        if count < 9:
            self.send(left, right)
        return self.came

    def full(self, *others):
        left, right = tie(self.came, *others)
        pieces = self.pieces + [left, right]
        whole = [shape((8,) + self.pieces[0].shape, B16)]
        if self.far:
            return call(
                assemble_far_kernel, self.name + "_assemble", [self.meta, *pieces], whole,
                scratch=[pltpu.SemaphoreType.DMA((9,))], raw=range(1, 10),
            )[0]
        return call(assemble_kernel, self.name + "_assemble", [self.meta, *pieces], whole)[0]


def gather_four(rows):
    far = swap(rows, "rep", 2)
    near = swap(rows, "rep", 1)
    diag = swap(far, "rep", 1)
    return [rows, near, far, diag]


def pass_far(give3, give1, keep2):
    came = swap(give3, "rep", 1)
    near = swap(give1, "rep", 1)
    (summed,) = call(add_far_kernel, "add_far", [keep2, came], [shape(keep2.shape, B16)])
    return near, swap(summed, "rep", 2), summed


class Halving:
    def __init__(self, name, meta, term, give):
        self.name, self.meta, self.term = name, meta, term
        self.came = (swap(give[0], "seq", 1), swap(give[1], "seq", 2))

    def one(self, *others):
        rows, cols = self.term.shape[3] // 2, self.term.shape[4]
        outs = [shape((2, rows, cols), F32)] * 2 + [shape((2, rows, cols), B16)] * 2
        args = [self.meta, self.term, *tie(self.came, *others)]
        *self.keep, ga, gb = call(halve_one_kernel, self.name + "_one", args, outs)
        self.came = (swap(ga, "seq", 2), swap(gb, "seq", 1))
        return ga

    def two_kept(self, *others):
        rows, cols = self.term.shape[3] // 2, self.term.shape[4]
        outs = [shape((rows, cols), F32)] * 2 + [shape((rows, cols), B16)] * 2
        args = [self.meta, *self.keep, *tie(self.came, *others)]
        return call(halve_two_kernel, self.name + "_two", args, outs)

    def two(self, *others):
        *self.keep, ga, gb = self.two_kept(*others)
        self.came = (swap(ga, "seq", 4), swap(gb, "seq", 4))
        return ga

    def last(self, *others):
        return [*self.keep, *tie(self.came, *others)]


def exchange(blocks):
    return lax.all_to_all(blocks, "seq", 0, 0, tiled=True)


def per_device_fast(
    tokens,
    cotangent,
    lengths,
    in_weight,
    in_bias,
    short_taps,
    short_bias,
    feat_weight,
    feat_bias,
    inner_weight,
    inner_bias,
    deep_weight,
    deep_bias,
    sine_freq,
    kernel_weight,
    skip_gain,
    out_weight,
    out_bias,
    norm1_gain,
    norm1_shift,
    norm2_gain,
    norm2_shift,
    up_weight,
    up_bias,
    down_weight,
    down_bias,
):
    tok_rows, model = tokens.shape
    group = tok_rows * 4
    blocks = 4
    seq_len = blocks * group
    chan = model // 32
    width = model // 4
    hidden = up_weight.shape[2]
    owned = model // 8
    filt = feat_weight.shape[2]
    device = lax.axis_index("seq") * 4 + lax.axis_index("rep")
    meta = lax.dynamic_index_in_dim(jnp.asarray(meta_table(group)), device, 0, keepdims=False)
    row_f32, row_b16 = shape((tok_rows, model), F32), shape((tok_rows, model), B16)
    sums_shapes = [row_b16, row_b16, row_f32, row_f32]
    flat_shape = shape((width, group), B16)

    normed, io_shard = call(
        start_kernel,
        "start",
        [tokens, norm1_gain, norm1_shift, in_weight[0].transpose(1, 0, 2), out_weight],
        [row_b16, shape((owned, 4 * width), B16)],
        away=range(5),
        limit=62,
    )
    io_ring = RingGather("io", meta, io_shard)
    x_one = gather_four(normed)
    twist, table = transform_tables(blocks, group)
    hi, lo = split_table(table)
    grid, ramp = feature_table(seq_len, feat_weight.shape[1])
    twist, grid, ramp = jnp.asarray(twist), jnp.asarray(grid), jnp.asarray(ramp)
    params = [
        cotangent, up_weight, down_weight,
        short_taps.transpose(1, 2, 0, 3), short_bias.transpose(1, 0, 2), in_bias.transpose(1, 0, 2), up_bias, skip_gain,
        jnp.asarray(decay_rates(model).T), kernel_weight, feat_weight.transpose(1, 0, 2),
        feat_bias, inner_bias, deep_bias, sine_freq,
    ]
    top_rows, ud_shard, cols, up_block, chans, columns, small_col, small_row, feat = call(
        setup_kernel,
        "setup",
        [meta, lengths, *params],
        [
            row_b16, shape((2, owned, hidden), B16),
            shape((width, 16), F32), shape((1, hidden), F32), shape((chan, 2), F32), shape((filt, chan), F32),
            shape((filt, 4), F32), shape((4, filt), F32), shape(feat_weight.shape[1:], F32),
        ],
        scratch=[pltpu.SemaphoreType.DMA((2,))],
        away=[2] + list(range(5, 2 + len(params))),
        raw=[3, 4, -2],
    )
    io_ring.step(x_one[1])
    tables = [grid, ramp, inner_weight, deep_weight, twist, hi, lo]
    kern_spec, sines, cosines = call(
        filter_ahead_kernel,
        "filter_ahead",
        [chans, feat, tie(small_col, io_ring.pieces[-1]), columns, *tables],
        [
            shape((blocks * chan, 2 * group), F32),
            shape((3, filt, seq_len), F32),
            shape((3, filt, seq_len), F32),
        ],
        scratch=[pltpu.VMEM((blocks * chan, 2 * group), F32)],
        away=range(4, 4 + len(tables)),
    )
    io_ring.step(kern_spec, x_one[2])

    edge = shape((HALO, model), B16)
    last, first = call(edges_kernel, "edges", [meta, *x_one], [edge, edge])
    before = lax.ppermute(last, "seq", [(i, (i + 1) % 8) for i in range(8)])
    after = lax.ppermute(first, "seq", [(i, (i + 7) % 8) for i in range(8)])
    io_ring.step()
    io_pieces = io_ring.pieces + list(tie(io_ring.came, before, after))
    ud_ring = RingGather("ud", meta, tie(ud_shard, io_pieces[-1]))
    g_top = gather_four(tie(top_rows, x_one[3]))
    full_io, proj, halo, gated = call(
        project_kernel,
        "project",
        [meta, lengths, *x_one, before, after, cols, *io_pieces],
        [
            shape((8, owned, 4 * width), B16), shape((3, width, group), B16), shape((3, width, 2 * LANE), B16), flat_shape
        ],
    )
    full_io = full_io.reshape(model, 4 * width)
    common = [proj, halo, cols]

    spread = (8, chan, group)
    received = exchange(gated.reshape(spread))
    spec_rows = 2 * blocks * chan
    mixed, kept_spec = call(
        conv_ahead_kernel,
        "conv_ahead",
        [kern_spec, twist, hi, lo, chans, received],
        [shape(spread, B16), shape((spec_rows, 2 * group), F32)],
        scratch=[pltpu.VMEM((spec_rows, 2 * group), F32)],
    )
    ud_ring.step(mixed)
    mixed = exchange(mixed).reshape(width, group)
    ud_ring.step(mixed)

    y_tok, give3, give1, keep2, keep0 = call(
        out_project_kernel,
        "out_project",
        [meta, lengths, *common, full_io, mixed],
        [shape((4, tok_rows, width), B16)] + sums_shapes,
    )
    near, far, _ = pass_far(give3, give1, keep2)
    middle, normed_two = call(
        norm_second_kernel,
        "norm_second",
        [tokens, keep0, near, far, out_bias, norm2_gain, norm2_shift],
        [row_f32, row_b16],
    )
    ud_ring.step(normed_two)
    x_two = gather_four(normed_two)
    full_ud = ud_ring.full(x_two[2])

    tall = shape((group, hidden), B16)
    act, gpre, gup = call(
        mlp_kernel, "mlp", [*x_two, *g_top, full_ud, up_block], [tall, tall, shape((1, hidden), F32)],
    )
    give3, give1, keep2, keep0 = call(partial(rows_kernel, 0), "grad_two", [gpre, full_ud], sums_shapes)
    near, far, passed = pass_far(give3, give1, keep2)
    give = shape((2, 2, owned, hidden), B16)
    mlp_terms, ga, gb = call(
        mlp_grad_kernel,
        "mlp_grad",
        [meta, *x_two, *g_top, act, tie(gpre, passed)],
        [shape((2, 2, 2, 2 * owned, hidden), B16), give, give],
    )
    wide_back = Halving("far", meta, mlp_terms, (ga, gb))
    grad_middle, gx, norm_sums = call(
        norm_second_back_kernel,
        "norm_second_back",
        [meta, lengths, keep0, near, tie(far, ga), middle, cotangent, norm2_gain],
        [row_f32, row_b16, shape((8, model), F32)],
    )
    g_mid = gather_four(gx)
    m3, m1, m2, m0 = call(partial(rows_kernel, 1), "mlp_rows", [tie(act, gx), full_ud], sums_shapes)
    gy, gate_first, gmix = call(
        grad_gate_kernel,
        "grad_gate",
        [meta, lengths, *tie(tuple(g_mid), m3), full_io, *common, mixed],
        [flat_shape, shape((width, LANE), F32), flat_shape],
    )

    received = exchange(gmix.reshape(spread))
    given = wide_back.one(received)
    gate_next = lax.ppermute(tie(gate_first, received), "seq", [(i, (i + 7) % 8) for i in range(8)])
    ggated, grad_kernel = call(
        conv_back_kernel,
        "conv_back",
        [kept_spec, kern_spec, twist, hi, lo, chans, tie(received, given)],
        [shape(spread, B16), shape((blocks, chan, group), F32)],
        scratch=[pltpu.VMEM((spec_rows, 2 * group), F32), pltpu.VMEM((3 * spec_rows // 2, 2 * group), F32)],
    )
    ggated = exchange(tie(ggated, gate_next)).reshape(width, group)
    up_keep, down_keep, up_give, down_give = wide_back.two_kept(ggated)
    up_came = swap(up_give, "seq", 4)
    (heads,) = call(heads_kernel, "heads", [tie(ggated, up_give)], [shape((width, LANE), B16)])
    ggated_next = lax.ppermute(heads, "seq", [(i, (i + 7) % 8) for i in range(8)])
    tok_first, sum_first, part_first = call(
        grad_first_kernel,
        "grad_first",
        [meta, lengths, *common, mixed, gy, tie(gate_next, heads), full_io],
        [shape((4, tok_rows, width), B16), shape((8, width), F32), shape((group, model), F32)],
    )
    cube = shape((2, 2, 2, owned, 2 * width), B16)
    give = shape((2, 2, owned // 2, 2 * width), B16)
    early_terms, ga, gb = call(
        grad_early_kernel,
        "grad_early",
        [meta, *g_mid, y_tok, *x_one, tok_first],
        [cube, give, give],
    )
    early = Halving("early", meta, early_terms, (ga, gb))
    tok_rest, col_sums, norm_one, give3, give1, keep2, keep0 = call(
        grad_short_kernel,
        "grad_short",
        [
            meta, lengths, *common, gy, full_io, part_first, *x_one, norm1_gain, norm1_shift, tie(ggated, ga),
            ggated_next
        ],
        [shape((4, tok_rows, 2 * width), B16), shape((16, width), F32), shape((2, model), F32)] + sums_shapes,
    )
    result = shape((1, owned, hidden), F32)
    down_came = swap(tie(down_give, give3), "seq", 4)
    (grad_up,) = call(add_last_kernel, "up_last", [up_keep, tie(up_came, give3)], [result])
    given = early.one(grad_up)
    near, far, passed = pass_far(give3, give1, tie(keep2, given))
    late_terms, ga, gb = call(
        grad_late_kernel, "grad_late", [meta, *tie(tuple(x_one), passed), tok_rest], [cube, give, give]
    )
    late = Halving("late", meta, late_terms, (ga, gb))
    side, wide = call(
        filter_back_kernel,
        "filter_back",
        [
            meta, tie(grad_kernel, ga), grid, ramp, chans, feat, inner_weight, deep_weight, small_col, small_row, columns,
            sines, cosines
        ],
        [shape((filt, 4 * filt), F32), shape((filt, width), F32)],
    )

    (small,) = call(
        pack_small_kernel,
        "pack_small",
        [side, wide, sum_first, col_sums, gup, norm_one, norm_sums],
        [shape((2 * HALF, width), F32)],
    )
    came = swap(small, "seq", 1)
    (grad_down,) = call(add_last_kernel, "down_last", [down_keep, tie(down_came, small)], [result])
    given = early.two(grad_down)
    (grad_tokens,) = call(
        norm_first_back_kernel,
        "norm_first_back",
        [keep0, near, tie(far, given), tokens, grad_middle, norm1_gain],
        [row_f32],
    )
    given = late.one(grad_tokens)
    (small,) = call(add_small_kernel, "add_small", [small, tie(came, given)], [small])
    came = swap(small, "seq", 2)
    given = late.two(small)
    m_near, m_far, m_passed = pass_far(tie(m3, given), m1, m2)
    grad_out, first_in = call(
        early_last_kernel, "early_last", early.last(given), [shape((1, owned, width), F32), shape((owned, width), F32)]
    )
    (small,) = call(add_small_kernel, "add_small", [small, tie(came, grad_out, m_passed)], [small])
    came = swap(small, "seq", 4)
    (grad_in,) = call(
        late_last_kernel, "late_last", [*late.last(small), first_in], [shape((1, 3, owned, width), F32)]
    )
    (small,) = call(add_small_kernel, "add_small", [small, tie(came, grad_in)], [small])
    came = swap(small, "rep", 2)
    (layer_out,) = call(layer_out_kernel, "layer_out", [m0, m_near, tie(m_far, small), middle, down_bias], [row_b16])
    (small,) = call(
        list_small_kernel, "list_small", [meta, small, tie(came, layer_out)], [shape((3 * HALF, width), F32)]
    )
    came = swap(small, "rep", 1)
    vector = shape((1, model), F32)
    square, short = shape((1, filt, filt), F32), shape((1, filt), F32)
    triple = shape((3, 1, model), F32)
    outs = call(
        unpack_small_kernel,
        "unpack_small",
        [meta, small, came],
        [
            triple, shape((3, 3, 1, model), F32), triple, shape(params[10].shape, F32), short, square, short, square,
            short, short, shape(kernel_weight.shape, F32), vector, vector, vector, vector, vector, vector,
            shape(up_bias.shape, F32), vector,
        ],
    )
    return (
        layer_out,
        grad_tokens,
        grad_in.transpose(0, 2, 1, 3),
        outs[0].transpose(1, 0, 2),
        outs[1].transpose(2, 0, 1, 3),
        outs[2].transpose(1, 0, 2),
        outs[3].transpose(1, 0, 2),
        *outs[4:12],
        grad_out,
        *outs[12:17],
        grad_up,
        outs[17],
        grad_down,
        outs[18],
    )


def solution(mesh):
    rows = P(("seq", "rep"), None)
    cut = P(None, "seq", "rep")
    wide = P(None, "seq", None, "rep")
    whole = P()
    ins = [rows, rows, whole, wide] + [whole] * 12 + [cut] + [whole] * 5 + [cut, whole, cut, whole]
    outs = [rows, rows, wide] + [whole] * 12 + [cut] + [whole] * 5 + [cut, whole, cut, whole]
    fast = mesh.shape["seq"] == 8 and mesh.shape["rep"] == 4
    return jax.shard_map(
        per_device_fast if fast else per_device, mesh=mesh, in_specs=tuple(ins), out_specs=tuple(outs), check_vma=False
    )
```

profile of v0, /device:TPU:0, one launch (start us, length us, event | category | flops | bytes accessed | tf_op | source)
XLA Modules:
  0.0 279.1 jit_solution(9557551716345241413)
XLA Ops:
  0.8 2.2 start.1
  3.0 3.0 %collective-permute-start.6 = (bf16[128,1024]{1,0:T(8,128)(2,1)}, bf16[128,1024]{1,0:T(8,128)(2,1)S(1)}, u32[]{:S(2)}, u32[]{:S(2)}) collective-permute-start(bf16[128,1024]{1,0:T(8,128)(2,1)} %get-tuple-element.211.refs_9_), channel_id=1, source_target_pairs={{8,0},{16,8},{24,16},{28,24},{20,28},{12,20},{4,12},{0,4},{9,1},{1... | collective-permute-start | bytes 786440 | tf_op jit(solution)/shard_map/ppermute | solution.py:1626
  16.1 5.0 %filter_ahead.1 = (f32[128,1024]{1,0:T(8,128)S(1)}, f32[3,64,2048]{2,1,0:T(8,128)S(1)}, f32[3,64,2048]{2,1,0:T(8,128)S(1)}) custom-call(f32[32,2]{1,0:T(8,128)S(1)} %get-tuple-element.214.refs_0_.refs_4_.refs_5_, f32[33,64]{1,0:T(8,128)S(1)} %get-tuple-element.215.refs_1_.refs_5_, f32[64,4]{1,0:T(8,128)S(1)} %get-tuple-element.217.refs_2_.refs_8_, ...), custom_call_target="tpu_custom_call" | custom-call | flops 6000000000 | bytes 100000 | tf_op jit(solution)/shard_map/filter_ahead/pallas_call | solution.py:959
  24.4 4.3 %collective-permute-done.9.refs_0_.refs_14_ = bf16[128,1024]{1,0:T(8,128)(2,1)S(1)} collective-permute-done((bf16[128,1024]{1,0:T(8,128)(2,1)S(1)}, bf16[128,1024]{1,0:T(8,128)(2,1)S(1)}, u32[]{:S(2)}, u32[]{:S(2)}) %collective-permute-start.9) | collective-permute-done | bytes 262176 | tf_op jit(solution)/shard_map/ppermute | solution.py:1626
  33.6 3.2 %collective-permute-start.4 = (bf16[16,1024]{1,0:T(8,128)(2,1)S(1)}, bf16[16,1024]{1,0:T(8,128)(2,1)S(1)}, u32[]{:S(2)}, u32[]{:S(2)}) collective-permute-start(bf16[16,1024]{1,0:T(8,128)(2,1)S(1)} %get-tuple-element.209), channel_id=1, source_target_pairs={{0,28},{4,0},{8,4},{12,8},{16,12},{20,16},{24,20},{28,24},{1,29},{... | collective-permute-start | bytes 98312 | tf_op jit(solution)/shard_map/ppermute | solution.py:1798
  43.7 3.4 %project.1 = (bf16[8,128,1024]{2,1,0:T(8,128)(2,1)S(1)}, bf16[3,256,512]{2,1,0:T(8,128)(2,1)S(1)}, bf16[3,256,256]{2,1,0:T(8,128)(2,1)S(1)}, bf16[256,512]{1,0:T(8,128)(2,1)S(1)}) custom-call(s32[34]{0:T(128)S(1)} %dynamic-slice_bitcast_fusion.refs_0_, s32[2]{0:T(128)S(1)} %copy-done.71, bf16[128,1024]{1,0:T(8,128)(2,1)S(1)} %copy-done.2, ...), custom_call_target="tpu_custom_call" | custom-call | flops 1000000 | bytes 100000 | tf_op jit(solution)/shard_map/project/pallas_call | solution.py:959
  47.1 14.9 %all_to_all.20.refs_5_ = bf16[8,32,512]{2,1,0:T(8,128)(2,1)S(1)} all-to-all(bf16[8,32,512]{2,1,0:T(8,128)(2,1)S(1)} %bitcast.26), channel_id=1, replica_groups=mesh['seq'=8,'rep'=4] {'seq'}, dimensions={0} | all-to-all | bytes 524288 | tf_op jit(solution)/shard_map/all_to_all | solution.py:1700
  62.0 4.0 %conv_ahead.1 = (bf16[8,32,512]{2,1,0:T(8,128)(2,1)S(1)}, f32[256,1024]{1,0:T(8,128)S(1)}) custom-call(f32[128,1024]{1,0:T(8,128)S(1)} %get-tuple-element.219.refs_0_.refs_1_, f32[4,4,2,512]{3,2,1,0:T(2,128)S(1)} %copy-done.42, bf16[1024,1024]{1,0:T(8,128)(2,1)S(1)} %copy-done.1, bf16[1024,1024]{1,0:T(8,128)(2,1)S(1)} %copy-done, ...), custom_call_target="tpu_custom_call" | custom-call | flops 1000000 | bytes 100000 | tf_op jit(solution)/shard_map/conv_ahead/pallas_call | solution.py:959
  68.1 10.6 %all_to_all.21 = bf16[8,32,512]{2,1,0:T(8,128)(2,1)S(1)} all-to-all(bf16[8,32,512]{2,1,0:T(8,128)(2,1)S(1)} %get-tuple-element.232), channel_id=1, replica_groups=mesh['seq'=8,'rep'=4] {'seq'}, dimensions={0} | all-to-all | bytes 524288 | tf_op jit(solution)/shard_map/all_to_all | solution.py:1700
  84.7 7.1 %collective-permute-done.15.refs_3_ = bf16[128,1024]{1,0:T(8,128)(2,1)S(1)} collective-permute-done((bf16[128,1024]{1,0:T(8,128)(2,1)S(1)}, bf16[128,1024]{1,0:T(8,128)(2,1)S(1)}, u32[]{:S(2)}, u32[]{:S(2)}) %collective-permute-start.15) | collective-permute-done | bytes 262176 | tf_op jit(solution)/shard_map/ppermute | solution.py:23
  98.4 4.2 %collective-permute-done.17.refs_2_.refs_3_ = bf16[128,1024]{1,0:T(8,128)(2,1)S(1)} collective-permute-done((bf16[128,1024]{1,0:T(8,128)(2,1)S(1)}, bf16[128,1024]{1,0:T(8,128)(2,1)S(1)}, u32[]{:S(2)}, u32[]{:S(2)}) %collective-permute-start.17) | collective-permute-done | bytes 262176 | tf_op jit(solution)/shard_map/ppermute | solution.py:23
  105.3 3.1 %mlp.1 = (bf16[512,1024]{1,0:T(8,128)(2,1)S(1)}, bf16[512,1024]{1,0:T(8,128)(2,1)S(1)}, f32[1,1024]{1,0:T(1,128)S(1)}) custom-call(bf16[128,1024]{1,0:T(8,128)(2,1)S(1)} %get-tuple-element.237.refs_0_.refs_1_, bf16[128,1024]{1,0:T(8,128)(2,1)S(1)} %collective-permute-done.16.refs_1_.refs_2_, bf16[128,1024]{1,0:T(8,128)(2,1)S(1)} %collective-permute-done.17.refs_2_.refs_3_, ...), custom_call_target="tpu_custom_call" | custom-call | flops 1000000 | bytes 100000 | tf_op jit(solution)/shard_map/mlp/pallas_call | solution.py:959
  112.9 3.4 %mlp_grad.1 = (bf16[2,2,2,256,1024]{4,3,2,1,0:T(8,128)(2,1)S(1)}, bf16[2,2,128,1024]{3,2,1,0:T(8,128)(2,1)S(1)}, bf16[2,2,128,1024]{3,2,1,0:T(8,128)(2,1)S(1)}) custom-call(s32[34]{0:T(128)S(1)} %dynamic-slice_bitcast_fusion.refs_0_, bf16[128,1024]{1,0:T(8,128)(2,1)S(1)} %get-tuple-element.237.refs_0_.refs_1_, ...), custom_call_target="tpu_custom_call" | custom-call | flops 1000000 | bytes 100000 | tf_op jit(solution)/shard_map/mlp_grad/pallas_call | solution.py:959
  116.3 3.4 %collective-permute-done.32.refs_4_ = bf16[128,1024]{1,0:T(8,128)(2,1)S(1)} collective-permute-done((bf16[128,1024]{1,0:T(8,128)(2,1)S(1)}, bf16[128,1024]{1,0:T(8,128)(2,1)S(1)}, u32[]{:S(2)}, u32[]{:S(2)}) %collective-permute-start.32) | collective-permute-done | bytes 262176 | tf_op jit(solution)/shard_map/ppermute | solution.py:23
  124.8 4.2 %collective-permute-done.35.refs_4_.refs_3_ = bf16[128,1024]{1,0:T(8,128)(2,1)S(1)} collective-permute-done((bf16[128,1024]{1,0:T(8,128)(2,1)S(1)}, bf16[128,1024]{1,0:T(8,128)(2,1)S(1)}, u32[]{:S(2)}, u32[]{:S(2)}) %collective-permute-start.35) | collective-permute-done | bytes 262176 | tf_op jit(solution)/shard_map/ppermute | solution.py:23
  132.4 20.0 %all_to_all.22.refs_6_ = bf16[8,32,512]{2,1,0:T(8,128)(2,1)S(1)} all-to-all(bf16[8,32,512]{2,1,0:T(8,128)(2,1)S(1)} %bitcast.27), channel_id=1, replica_groups=mesh['seq'=8,'rep'=4] {'seq'}, dimensions={0} | all-to-all | bytes 524288 | tf_op jit(solution)/shard_map/all_to_all | solution.py:1700
  152.4 13.2 %collective-permute-start.37 = (f32[256,128]{1,0:T(8,128)S(1)}, f32[256,128]{1,0:T(8,128)S(1)}, u32[]{:S(2)}, u32[]{:S(2)}) collective-permute-start(f32[256,128]{1,0:T(8,128)S(1)} %get-tuple-element.276), channel_id=1, source_target_pairs={{0,28},{4,0},{8,4},{12,8},{16,12},{20,16},{24,20},{28,24},{1,29},{... | collective-permute-start | bytes 393224 | tf_op jit(solution)/shard_map/ppermute | solution.py:1876
  170.0 4.9 %conv_back.1 = (bf16[8,32,512]{2,1,0:T(8,128)(2,1)S(1)}, f32[4,32,512]{2,1,0:T(8,128)S(1)}) custom-call(f32[256,1024]{1,0:T(8,128)S(1)} %get-tuple-element.277.refs_0_, f32[128,1024]{1,0:T(8,128)S(1)} %get-tuple-element.219.refs_0_.refs_1_, f32[4,4,2,512]{3,2,1,0:T(2,128)S(1)} %copy-done.42, bf16[1024,1024]{1,0:T(8,128)(2,1)S(1)} %copy-done.1, ...), custom_call_target="tpu_custom_call" | custom-call | flops 1000000 | bytes 100000 | tf_op jit(solution)/shard_map/conv_back/pallas_call | solution.py:959
  177.1 4.2 %all-to-all-start.3 = ((bf16[8,32,512]{2,1,0:T(8,128)(2,1)}), bf16[8,32,512]{2,1,0:T(8,128)(2,1)}, u32[]{:S(2)}, u32[]{:S(2)}) async-start(bf16[8,32,512]{2,1,0:T(8,128)(2,1)} %copy-done.52), calls=%async_computation.3 | async-start | bytes 524288 | tf_op jit(solution)/shard_map/all_to_all | solution.py:1700
  181.3 8.3 %all-to-all-done.3 = bf16[8,32,512]{2,1,0:T(8,128)(2,1)} async-done(((bf16[8,32,512]{2,1,0:T(8,128)(2,1)}), bf16[8,32,512]{2,1,0:T(8,128)(2,1)}, u32[]{:S(2)}, u32[]{:S(2)}) %all-to-all-start.3) | async-done | bytes 262176 | tf_op jit(solution)/shard_map/all_to_all | solution.py:1700
  197.0 2.7 grad_first.1
  202.2 5.6 %grad_short.1 = (bf16[4,128,512]{2,1,0:T(8,128)(2,1)S(1)}, f32[16,256]{1,0:T(8,128)S(1)}, f32[2,1024]{1,0:T(2,128)S(1)}, bf16[128,1024]{1,0:T(8,128)(2,1)S(1)}, ...) custom-call(s32[34]{0:T(128)S(1)} %dynamic-slice_bitcast_fusion.refs_0_, ...), custom_call_target="tpu_custom_call" | custom-call | flops 1000000 | bytes 100000 | tf_op jit(solution)/shard_map/grad_short/pallas_call | solution.py:959
  217.2 6.1 %collective-permute-done.53.refs_1_ = bf16[128,1024]{1,0:T(8,128)(2,1)S(1)} collective-permute-done((bf16[128,1024]{1,0:T(8,128)(2,1)S(1)}, bf16[128,1024]{1,0:T(8,128)(2,1)S(1)}, u32[]{:S(2)}, u32[]{:S(2)}) %collective-permute-start.53) | collective-permute-done | bytes 262176 | tf_op jit(solution)/shard_map/ppermute | solution.py:23
  224.8 3.5 %filter_back.1 = (f32[64,256]{1,0:T(8,128)S(1)}, f32[64,256]{1,0:T(8,128)S(1)}) custom-call(s32[34]{0:T(128)S(1)} %dynamic-slice_bitcast_fusion.refs_0_, f32[4,32,512]{2,1,0:T(8,128)S(1)} %copy-done.46, f32[33,2048]{1,0:T(8,128)S(1)} %copy-done.41, f32[1,2048]{1,0:T(1,128)S(1)} %copy-done.74, f32[32,2]{1,0:T(8,128)S(1)} %copy-done.56, ...), custom_call_target="tpu_custom_call" | custom-call | flops 1000000 | bytes 100000 | tf_op jit(solution)/shard_map/filter_back/pallas_call | solution.py:959
  228.4 3.0 %collective-permute-done.51.refs_3_ = bf16[2,64,512]{2,1,0:T(8,128)(2,1)S(1)} collective-permute-done((bf16[2,64,512]{2,1,0:T(8,128)(2,1)S(1)}, bf16[2,64,512]{2,1,0:T(8,128)(2,1)S(1)}, u32[]{:S(2)}, u32[]{:S(2)}) %collective-permute-start.51) | collective-permute-done | bytes 131104 | tf_op jit(solution)/shard_map/ppermute | solution.py:23
  237.9 2.5 collective-permute-done.55.refs_4_
  242.5 3.4 %collective-permute-start.61 = (bf16[64,512]{1,0:T(8,128)(2,1)S(1)}, bf16[64,512]{1,0:T(8,128)(2,1)S(1)}, u32[]{:S(2)}, u32[]{:S(2)}) collective-permute-start(bf16[64,512]{1,0:T(8,128)(2,1)S(1)} %get-tuple-element.356), channel_id=1, source_target_pairs={{0,16},{4,20},{8,24},{12,28},{16,0},{20,4},{24,8},{28,12},{1,17},{... | collective-permute-start | bytes 196616 | tf_op jit(solution)/shard_map/ppermute | solution.py:23
  246.0 3.0 %collective-permute-done.61.refs_3_ = bf16[64,512]{1,0:T(8,128)(2,1)S(1)} collective-permute-done((bf16[64,512]{1,0:T(8,128)(2,1)S(1)}, bf16[64,512]{1,0:T(8,128)(2,1)S(1)}, u32[]{:S(2)}, u32[]{:S(2)}) %collective-permute-start.61) | collective-permute-done | bytes 65568 | tf_op jit(solution)/shard_map/ppermute | solution.py:23
  248.9 4.9 %collective-permute-done.60.refs_2_ = bf16[64,512]{1,0:T(8,128)(2,1)S(1)} collective-permute-done((bf16[64,512]{1,0:T(8,128)(2,1)S(1)}, bf16[64,512]{1,0:T(8,128)(2,1)S(1)}, u32[]{:S(2)}, u32[]{:S(2)}) %collective-permute-start.60) | collective-permute-done | bytes 65568 | tf_op jit(solution)/shard_map/ppermute | solution.py:23
  255.3 2.8 %collective-permute-start.64 = (bf16[64,512]{1,0:T(8,128)(2,1)S(1)}, bf16[64,512]{1,0:T(8,128)(2,1)S(1)}, u32[]{:S(2)}, u32[]{:S(2)}) collective-permute-start(bf16[64,512]{1,0:T(8,128)(2,1)S(1)} %get-tuple-element.363), channel_id=1, source_target_pairs={{0,16},{4,20},{8,24},{12,28},{16,0},{20,4},{24,8},{28,12},{1,17},{... | collective-permute-start | bytes 196616 | tf_op jit(solution)/shard_map/ppermute | solution.py:23
  258.2 10.0 %collective-permute-done.64.refs_3_ = bf16[64,512]{1,0:T(8,128)(2,1)S(1)} collective-permute-done((bf16[64,512]{1,0:T(8,128)(2,1)S(1)}, bf16[64,512]{1,0:T(8,128)(2,1)S(1)}, u32[]{:S(2)}, u32[]{:S(2)}) %collective-permute-start.64) | collective-permute-done | bytes 65568 | tf_op jit(solution)/shard_map/ppermute | solution.py:23
  271.2 4.1 %collective-permute-done.65.refs_2_ = f32[176,256]{1,0:T(8,128)S(1)} collective-permute-done((f32[176,256]{1,0:T(8,128)S(1)}, f32[176,256]{1,0:T(8,128)S(1)}, u32[]{:S(2)}, u32[]{:S(2)}) %collective-permute-start.65) | collective-permute-done | bytes 180256 | tf_op jit(solution)/shard_map/ppermute | solution.py:23
  (356 shorter events, 98.8 us)
Async XLA Ops:
  3.0 9.6 %collective-permute-start.6 = (bf16[128,1024]{1,0:T(8,128)(2,1)}, bf16[128,1024]{1,0:T(8,128)(2,1)S(1)}, u32[]{:S(2)}, u32[]{:S(2)}) collective-permute-start(bf16[128,1024]{1,0:T(8,128)(2,1)} %get-tuple-element.211.refs_9_), channel_id=1, source_target_pairs={{8,0},{16,8},{24,16},{28,24},{20,28},{12,20},{4,12},{0,4},{9,1},{1... | collective-permute-start | bytes 786440 | tf_op jit(solution)/shard_map/ppermute | solution.py:1626
  6.1 16.2 %collective-permute-start.1 = (bf16[128,1024]{1,0:T(8,128)(2,1)}, bf16[128,1024]{1,0:T(8,128)(2,1)S(1)}, u32[]{:S(2)}, u32[]{:S(2)}) collective-permute-start(bf16[128,1024]{1,0:T(8,128)(2,1)} %get-tuple-element.309.refs_1_.refs_2_.refs_6_.refs_8_), channel_id=1, source_target_pairs={{0,2},{1,3},{2,0},{3,1},{4,6},{5,7},{6,4},{7,5},{8,10},{9,11},{10,... | collective-permute-start | bytes 786440 | tf_op jit(solution)/shard_map/ppermute | solution.py:23
  29.3 9.5 %collective-permute-start.11 = (bf16[64,1024]{1,0:T(8,128)(2,1)S(1)}, bf16[64,1024]{1,0:T(8,128)(2,1)S(1)}, u32[]{:S(2)}, u32[]{:S(2)}) collective-permute-start(bf16[64,1024]{1,0:T(8,128)(2,1)S(1)} %get-tuple-element.224), channel_id=1, source_target_pairs={{0,8},{8,16},{16,24},{24,28},{28,20},{20,12},{12,4},{4,0},{1,9},{9... | collective-permute-start | bytes 393224 | tf_op jit(solution)/shard_map/ppermute | solution.py:1626
  38.8 27.2 %collective-permute-start.23 = (bf16[2,128,1024]{2,1,0:T(8,128)(2,1)S(1)}, bf16[2,128,1024]{2,1,0:T(8,128)(2,1)S(1)}, u32[]{:S(2)}, u32[]{:S(2)}) collective-permute-start(bf16[2,128,1024]{2,1,0:T(8,128)(2,1)S(1)} %get-tuple-element.241.refs_1_), channel_id=1, source_target_pairs={{8,0},{16,8},{24,16},{28,24},{20,28},{12,20},{4,12},{0,4},{9,1},{1... | collective-permute-start | bytes 1572872 | tf_op jit(solution)/shard_map/ppermute | solution.py:1626
  40.3 25.7 %collective-permute-start.22 = (bf16[2,128,1024]{2,1,0:T(8,128)(2,1)S(1)}, bf16[2,128,1024]{2,1,0:T(8,128)(2,1)S(1)}, u32[]{:S(2)}, u32[]{:S(2)}) collective-permute-start(bf16[2,128,1024]{2,1,0:T(8,128)(2,1)S(1)} %get-tuple-element.241.refs_1_), channel_id=1, source_target_pairs={{0,8},{8,16},{16,24},{24,28},{28,20},{20,12},{12,4},{4,0},{1,9},{9... | collective-permute-start | bytes 1572872 | tf_op jit(solution)/shard_map/ppermute | solution.py:1626
  66.0 14.4 %collective-permute-start.24 = (bf16[2,128,1024]{2,1,0:T(8,128)(2,1)S(1)}, bf16[2,128,1024]{2,1,0:T(8,128)(2,1)S(1)}, u32[]{:S(2)}, u32[]{:S(2)}) collective-permute-start(bf16[2,128,1024]{2,1,0:T(8,128)(2,1)S(1)} %collective-permute-done.22.refs_2_), channel_id=1, source_target_pairs={{0,8},{8,16},{16,24},{24,28},{28,20},{20,12},{12,4},{4,0},{1,9},{9... | collective-permute-start | bytes 1572872 | tf_op jit(solution)/shard_map/ppermute | solution.py:1626
  66.1 14.3 %collective-permute-start.25 = (bf16[2,128,1024]{2,1,0:T(8,128)(2,1)S(1)}, bf16[2,128,1024]{2,1,0:T(8,128)(2,1)S(1)}, u32[]{:S(2)}, u32[]{:S(2)}) collective-permute-start(bf16[2,128,1024]{2,1,0:T(8,128)(2,1)S(1)} %collective-permute-done.23.refs_3_), channel_id=1, source_target_pairs={{8,0},{16,8},{24,16},{28,24},{20,28},{12,20},{4,12},{0,4},{9,1},{1... | collective-permute-start | bytes 1572872 | tf_op jit(solution)/shard_map/ppermute | solution.py:1626
  80.4 14.3 %collective-permute-start.26 = (bf16[2,128,1024]{2,1,0:T(8,128)(2,1)S(1)}, bf16[2,128,1024]{2,1,0:T(8,128)(2,1)S(1)}, u32[]{:S(2)}, u32[]{:S(2)}) collective-permute-start(bf16[2,128,1024]{2,1,0:T(8,128)(2,1)S(1)} %collective-permute-done.24.refs_4_), channel_id=1, source_target_pairs={{0,8},{8,16},{16,24},{24,28},{28,20},{20,12},{12,4},{4,0},{1,9},{9... | collective-permute-start | bytes 1572872 | tf_op jit(solution)/shard_map/ppermute | solution.py:1626
  81.4 14.0 %collective-permute-start.27 = (bf16[2,128,1024]{2,1,0:T(8,128)(2,1)S(1)}, bf16[2,128,1024]{2,1,0:T(8,128)(2,1)S(1)}, u32[]{:S(2)}, u32[]{:S(2)}) collective-permute-start(bf16[2,128,1024]{2,1,0:T(8,128)(2,1)S(1)} %collective-permute-done.25.refs_5_), channel_id=1, source_target_pairs={{8,0},{16,8},{24,16},{28,24},{20,28},{12,20},{4,12},{0,4},{9,1},{1... | collective-permute-start | bytes 1572872 | tf_op jit(solution)/shard_map/ppermute | solution.py:1626
  84.2 13.6 %collective-permute-start.20 = (bf16[128,1024]{1,0:T(8,128)(2,1)S(1)}, bf16[128,1024]{1,0:T(8,128)(2,1)S(1)}, u32[]{:S(2)}, u32[]{:S(2)}) collective-permute-start(bf16[128,1024]{1,0:T(8,128)(2,1)S(1)} %get-tuple-element.239.refs_4_.refs_5_), channel_id=1, source_target_pairs={{0,2},{1,3},{2,0},{3,1},{4,6},{5,7},{6,4},{7,5},{8,10},{9,11},{10,... | collective-permute-start | bytes 786440 | tf_op jit(solution)/shard_map/ppermute | solution.py:23
  92.1 10.5 %collective-permute-start.17 = (bf16[128,1024]{1,0:T(8,128)(2,1)S(1)}, bf16[128,1024]{1,0:T(8,128)(2,1)S(1)}, u32[]{:S(2)}, u32[]{:S(2)}) collective-permute-start(bf16[128,1024]{1,0:T(8,128)(2,1)S(1)} %get-tuple-element.237.refs_0_.refs_1_), channel_id=1, source_target_pairs={{0,2},{1,3},{2,0},{3,1},{4,6},{5,7},{6,4},{7,5},{8,10},{9,11},{10,... | collective-permute-start | bytes 786440 | tf_op jit(solution)/shard_map/ppermute | solution.py:23
  123.1 42.5 %collective-permute-start.39 = (bf16[2,2,128,1024]{3,2,1,0:T(8,128)(2,1)S(1)}, bf16[2,2,128,1024]{3,2,1,0:T(8,128)(2,1)S(1)}, u32[]{:S(2)}, u32[]{:S(2)}) collective-permute-start(bf16[2,2,128,1024]{3,2,1,0:T(8,128)(2,1)S(1)} %get-tuple-element.279), channel_id=1, source_target_pairs={{0,8},{4,12},{8,0},{12,4},{16,24},{20,28},{24,16},{28,20},{1,9},{5... | collective-permute-start | bytes 3145736 | tf_op jit(solution)/shard_map/ppermute | solution.py:23
  124.0 41.6 %collective-permute-start.38 = (bf16[2,2,128,1024]{3,2,1,0:T(8,128)(2,1)S(1)}, bf16[2,2,128,1024]{3,2,1,0:T(8,128)(2,1)S(1)}, u32[]{:S(2)}, u32[]{:S(2)}) collective-permute-start(bf16[2,2,128,1024]{3,2,1,0:T(8,128)(2,1)S(1)} %get-tuple-element.260), channel_id=1, source_target_pairs={{0,4},{4,0},{8,12},{12,8},{16,20},{20,16},{24,28},{28,24},{1,5},{5... | collective-permute-start | bytes 3145736 | tf_op jit(solution)/shard_map/ppermute | solution.py:23
  152.4 24.0 %collective-permute-start.37 = (f32[256,128]{1,0:T(8,128)S(1)}, f32[256,128]{1,0:T(8,128)S(1)}, u32[]{:S(2)}, u32[]{:S(2)}) collective-permute-start(f32[256,128]{1,0:T(8,128)S(1)} %get-tuple-element.276), channel_id=1, source_target_pairs={{0,28},{4,0},{8,4},{12,8},{16,12},{20,16},{24,20},{28,24},{1,29},{... | collective-permute-start | bytes 393224 | tf_op jit(solution)/shard_map/ppermute | solution.py:1876
  168.3 13.0 %collective-permute-start.41 = (bf16[2,128,1024]{2,1,0:T(8,128)(2,1)}, bf16[2,128,1024]{2,1,0:T(8,128)(2,1)}, u32[]{:S(2)}, u32[]{:S(2)}) collective-permute-start(bf16[2,128,1024]{2,1,0:T(8,128)(2,1)} %get-tuple-element.288), channel_id=1, source_target_pairs={{0,4},{4,0},{8,12},{12,8},{16,20},{20,16},{24,28},{28,24},{1,5},{5... | collective-permute-start | bytes 1572872 | tf_op jit(solution)/shard_map/ppermute | solution.py:23
  169.2 12.1 %collective-permute-start.40 = (bf16[2,128,1024]{2,1,0:T(8,128)(2,1)}, bf16[2,128,1024]{2,1,0:T(8,128)(2,1)}, u32[]{:S(2)}, u32[]{:S(2)}) collective-permute-start(bf16[2,128,1024]{2,1,0:T(8,128)(2,1)} %get-tuple-element.282), channel_id=1, source_target_pairs={{0,8},{4,12},{8,0},{12,4},{16,24},{20,28},{24,16},{28,20},{1,9},{5... | collective-permute-start | bytes 1572872 | tf_op jit(solution)/shard_map/ppermute | solution.py:23
  177.1 12.5 %all-to-all-start.3 = ((bf16[8,32,512]{2,1,0:T(8,128)(2,1)}), bf16[8,32,512]{2,1,0:T(8,128)(2,1)}, u32[]{:S(2)}, u32[]{:S(2)}) async-start(bf16[8,32,512]{2,1,0:T(8,128)(2,1)} %copy-done.52), calls=%async_computation.3 | async-start | bytes 524288 | tf_op jit(solution)/shard_map/all_to_all | solution.py:1700
  196.2 13.6 %collective-permute-start.45 = (bf16[128,1024]{1,0:T(8,128)(2,1)S(1)}, bf16[128,1024]{1,0:T(8,128)(2,1)S(1)}, u32[]{:S(2)}, u32[]{:S(2)}) collective-permute-start(bf16[128,1024]{1,0:T(8,128)(2,1)S(1)} %get-tuple-element.291), channel_id=1, source_target_pairs={{0,16},{4,20},{8,24},{12,28},{16,0},{20,4},{24,8},{28,12},{1,17},{... | collective-permute-start | bytes 786440 | tf_op jit(solution)/shard_map/ppermute | solution.py:23
  201.4 9.3 %collective-permute-start.44 = (bf16[2,2,64,512]{3,2,1,0:T(8,128)(2,1)S(1)}, bf16[2,2,64,512]{3,2,1,0:T(8,128)(2,1)S(1)}, u32[]{:S(2)}, u32[]{:S(2)}) collective-permute-start(bf16[2,2,64,512]{3,2,1,0:T(8,128)(2,1)S(1)} %get-tuple-element.301), channel_id=1, source_target_pairs={{0,8},{4,12},{8,0},{12,4},{16,24},{20,28},{24,16},{28,20},{1,9},{5... | collective-permute-start | bytes 786440 | tf_op jit(solution)/shard_map/ppermute | solution.py:23
  207.9 15.3 %collective-permute-start.53 = (bf16[128,1024]{1,0:T(8,128)(2,1)S(1)}, bf16[128,1024]{1,0:T(8,128)(2,1)S(1)}, u32[]{:S(2)}, u32[]{:S(2)}) collective-permute-start(bf16[128,1024]{1,0:T(8,128)(2,1)S(1)} %get-tuple-element.324), channel_id=1, source_target_pairs={{0,16},{4,20},{8,24},{12,28},{16,0},{20,4},{24,8},{28,12},{1,17},{... | collective-permute-start | bytes 786440 | tf_op jit(solution)/shard_map/ppermute | solution.py:23
  211.5 13.1 %collective-permute-start.52 = (bf16[2,64,512]{2,1,0:T(8,128)(2,1)S(1)}, bf16[2,64,512]{2,1,0:T(8,128)(2,1)S(1)}, u32[]{:S(2)}, u32[]{:S(2)}) collective-permute-start(bf16[2,64,512]{2,1,0:T(8,128)(2,1)S(1)} %get-tuple-element.321), channel_id=1, source_target_pairs={{0,4},{4,0},{8,12},{12,8},{16,20},{20,16},{24,28},{28,24},{1,5},{5... | collective-permute-start | bytes 393224 | tf_op jit(solution)/shard_map/ppermute | solution.py:23
  213.2 19.6 %collective-permute-start.49 = (bf16[128,1024]{1,0:T(8,128)(2,1)S(1)}, bf16[128,1024]{1,0:T(8,128)(2,1)S(1)}, u32[]{:S(2)}, u32[]{:S(2)}) collective-permute-start(bf16[128,1024]{1,0:T(8,128)(2,1)S(1)} %get-tuple-element.318), channel_id=1, source_target_pairs={{0,1},{1,0},{2,3},{3,2},{4,5},{5,4},{6,7},{7,6},{8,9},{9,8},{10,11... | collective-permute-start | bytes 786440 | tf_op jit(solution)/shard_map/ppermute | solution.py:23
  213.2 19.5 %collective-permute-start.50 = (bf16[128,1024]{1,0:T(8,128)(2,1)S(1)}, bf16[128,1024]{1,0:T(8,128)(2,1)S(1)}, u32[]{:S(2)}, u32[]{:S(2)}) collective-permute-start(bf16[128,1024]{1,0:T(8,128)(2,1)S(1)} %add_far.6), channel_id=1, source_target_pairs={{0,2},{1,3},{2,0},{3,1},{4,6},{5,7},{6,4},{7,5},{8,10},{9,11},{10,... | collective-permute-start | bytes 786440 | tf_op jit(solution)/shard_map/ppermute | solution.py:23
  215.1 18.9 %collective-permute-start.48 = (bf16[2,2,64,512]{3,2,1,0:T(8,128)(2,1)S(1)}, bf16[2,2,64,512]{3,2,1,0:T(8,128)(2,1)S(1)}, u32[]{:S(2)}, u32[]{:S(2)}) collective-permute-start(bf16[2,2,64,512]{3,2,1,0:T(8,128)(2,1)S(1)} %get-tuple-element.316), channel_id=1, source_target_pairs={{0,8},{4,12},{8,0},{12,4},{16,24},{20,28},{24,16},{28,20},{1,9},{5... | collective-permute-start | bytes 786440 | tf_op jit(solution)/shard_map/ppermute | solution.py:23
  223.2 10.8 %collective-permute-start.47 = (bf16[2,2,64,512]{3,2,1,0:T(8,128)(2,1)S(1)}, bf16[2,2,64,512]{3,2,1,0:T(8,128)(2,1)S(1)}, u32[]{:S(2)}, u32[]{:S(2)}) collective-permute-start(bf16[2,2,64,512]{3,2,1,0:T(8,128)(2,1)S(1)} %get-tuple-element.315), channel_id=1, source_target_pairs={{0,4},{4,0},{8,12},{12,8},{16,20},{20,16},{24,28},{28,24},{1,5},{5... | collective-permute-start | bytes 786440 | tf_op jit(solution)/shard_map/ppermute | solution.py:23
  242.4 12.1 %collective-permute-start.57 = (bf16[128,1024]{1,0:T(8,128)(2,1)S(1)}, bf16[128,1024]{1,0:T(8,128)(2,1)S(1)}, u32[]{:S(2)}, u32[]{:S(2)}) collective-permute-start(bf16[128,1024]{1,0:T(8,128)(2,1)S(1)} %copy-done.89), channel_id=1, source_target_pairs={{0,1},{1,0},{2,3},{3,2},{4,5},{5,4},{6,7},{7,6},{8,9},{9,8},{10,11... | collective-permute-start | bytes 786440 | tf_op jit(solution)/shard_map/ppermute | solution.py:23
  242.5 12.1 %collective-permute-start.59 = (f32[176,256]{1,0:T(8,128)S(1)}, f32[176,256]{1,0:T(8,128)S(1)}, u32[]{:S(2)}, u32[]{:S(2)}) collective-permute-start(f32[176,256]{1,0:T(8,128)S(1)} %add_small.3.refs_0_), channel_id=1, source_target_pairs={{0,8},{4,12},{8,0},{12,4},{16,24},{20,28},{24,16},{28,20},{1,9},{5... | collective-permute-start | bytes 540680 | tf_op jit(solution)/shard_map/ppermute | solution.py:23
  254.6 15.1 %collective-permute-start.62 = (f32[176,256]{1,0:T(8,128)S(1)}, f32[176,256]{1,0:T(8,128)S(1)}, u32[]{:S(2)}, u32[]{:S(2)}) collective-permute-start(f32[176,256]{1,0:T(8,128)S(1)} %add_small.4.refs_0_), channel_id=1, source_target_pairs={{0,16},{4,20},{8,24},{12,28},{16,0},{20,4},{24,8},{28,12},{1,17},{... | collective-permute-start | bytes 540680 | tf_op jit(solution)/shard_map/ppermute | solution.py:23
  254.7 15.7 %collective-permute-start.58 = (bf16[128,1024]{1,0:T(8,128)(2,1)S(1)}, bf16[128,1024]{1,0:T(8,128)(2,1)S(1)}, u32[]{:S(2)}, u32[]{:S(2)}) collective-permute-start(bf16[128,1024]{1,0:T(8,128)(2,1)S(1)} %add_far.7), channel_id=1, source_target_pairs={{0,2},{1,3},{2,0},{3,1},{4,6},{5,7},{6,4},{7,5},{8,10},{9,11},{10,... | collective-permute-start | bytes 786440 | tf_op jit(solution)/shard_map/ppermute | solution.py:23
  255.3 15.0 %collective-permute-start.33 = (bf16[128,1024]{1,0:T(8,128)(2,1)S(1)}, bf16[128,1024]{1,0:T(8,128)(2,1)S(1)}, u32[]{:S(2)}, u32[]{:S(2)}) collective-permute-start(bf16[128,1024]{1,0:T(8,128)(2,1)S(1)} %copy-done.87), channel_id=1, source_target_pairs={{0,1},{1,0},{2,3},{3,2},{4,5},{5,4},{6,7},{7,6},{8,9},{9,8},{10,11... | collective-permute-start | bytes 786440 | tf_op jit(solution)/shard_map/ppermute | solution.py:23
  255.3 12.9 %collective-permute-start.64 = (bf16[64,512]{1,0:T(8,128)(2,1)S(1)}, bf16[64,512]{1,0:T(8,128)(2,1)S(1)}, u32[]{:S(2)}, u32[]{:S(2)}) collective-permute-start(bf16[64,512]{1,0:T(8,128)(2,1)S(1)} %get-tuple-element.363), channel_id=1, source_target_pairs={{0,16},{4,20},{8,24},{12,28},{16,0},{20,4},{24,8},{28,12},{1,17},{... | collective-permute-start | bytes 196616 | tf_op jit(solution)/shard_map/ppermute | solution.py:23
  258.2 10.8 %collective-permute-start.63 = (bf16[64,512]{1,0:T(8,128)(2,1)S(1)}, bf16[64,512]{1,0:T(8,128)(2,1)S(1)}, u32[]{:S(2)}, u32[]{:S(2)}) collective-permute-start(bf16[64,512]{1,0:T(8,128)(2,1)S(1)} %get-tuple-element.352), channel_id=1, source_target_pairs={{0,16},{4,20},{8,24},{12,28},{16,0},{20,4},{24,8},{28,12},{1,17},{... | collective-permute-start | bytes 196616 | tf_op jit(solution)/shard_map/ppermute | solution.py:23
  (137 other events, 1399.3 us)
where the time goes:
time: 281 us; the launch traced here: 279 us
  waiting for transfers between devices  80.5 us (29%)
  starting transfers between devices  74.2 us (26%)
  Pallas kernels  64 us (23%)
  blocking collectives  45.5 us (16%)
  local copies, waits for them, and re-layouts  12.6 us (4%)
    pallas_call x46, Pallas kernels, call(): pl.pallas_call(body, out_shape=outs, in_specs=[space(i, a) for i, a in en...  64 us
    ppermute x47, waiting for transfers between devices, swap(): return lax.ppermute(values, axis_name, [(i, i ^ bit) for i in range(size)])  58.6 us
    all_to_all x3, blocking collectives, exchange(): return lax.all_to_all(blocks, 'seq', 0, 0, tiled=True)  45.5 us
    ppermute x47, starting transfers between devices, swap(): return lax.ppermute(values, axis_name, [(i, i ^ bit) for i in range(size)])  32.3 us
    ppermute x1, starting transfers between devices, per_device_fast(): lax.ppermute(tie(gate_first, received), 'seq', [(i, (i + 7) % 8) for i in...  13.2 us
    ppermute x8, starting transfers between devices, send(): lax.ppermute(right, 'seq', BACK)  12.2 us
    unnamed x202, local copies, waits for them, and re-layouts  11.9 us
    all_to_all x1, waiting for transfers between devices, exchange(): return lax.all_to_all(blocks, 'seq', 0, 0, tiled=True)  8.31 us
  transfers between devices with their start and end apart: 68, of which 26 were waited for; matrix products, arithmetic and copies ran while one was open for 0% of the time, Pallas kernels for 18%

commit v1 on v0

--- a/solution.py
+++ b/solution.py
@@ -366,6 +366,13 @@
     return dot(top, hi) + dot(rest, hi) + dot(top, lo)
 
 
+def dot_twice(values, hi, dims):
+    top = values.astype(B16)
+    rest = (values - top.astype(F32)).astype(B16)
+    dot = partial(lax.dot_general, dimension_numbers=(dims, ((), ())), preferred_element_type=F32)
+    return dot(top, hi) + dot(rest, hi)
+
+
 def turn_rows(blocks_in, twist_ref, z_ref, base, classes):
     rows, length = blocks_in[0].shape
     for q in range(classes):
@@ -396,11 +403,11 @@
     second = [x_ref[blocks + b].astype(F32) for b in range(short_blocks)]
     turn_rows(first, twist_ref, z_ref, 0, blocks)
     turn_rows(second, twist_ref, z_ref, span, blocks)
-    spec = dot_split(z_ref[...], hi_ref[...], lo_ref[...], ((1,), (0,)))
+    spec = dot_twice(z_ref[...], hi_ref[...], ((1,), (0,)))
     spec_ref[...] = spec
     kern = kern_ref[...]
     prod = jnp.concatenate([times(spec[:span], kern, False), times(spec[span:], kern, False)], axis=0)
-    w = dot_split(prod, hi_ref[...], lo_ref[...], ((1,), (1,)))
+    w = dot_twice(prod, hi_ref[...], ((1,), (1,)))
     skip = skip_ref[...]
     for b in range(blocks):
         out_ref[b] = (back_rows(w, 0, rows, b, twist_ref, blocks) + skip * first[b]).astype(B16)
@@ -1271,12 +1278,12 @@
     second = [g_ref[blocks + b].astype(F32) for b in range(short_blocks)]
     turn_rows(first, twist_ref, z_ref, 0, blocks)
     turn_rows(second, twist_ref, z_ref, span, blocks)
-    grad = dot_split(z_ref[...], hi_ref[...], lo_ref[...], ((1,), (0,)))
+    grad = dot_twice(z_ref[...], hi_ref[...], ((1,), (0,)))
     kern = kern_ref[...]
     p_ref[0:span] = times(grad[:span], kern, True)
     p_ref[span : 2 * span] = times(grad[span:], kern, True)
     p_ref[2 * span :] = times(grad[:span], spec_ref[0:span], True) + times(grad[span:], spec_ref[span:], True)
-    w = dot_split(p_ref[...], hi_ref[...], lo_ref[...], ((1,), (1,)))
+    w = dot_twice(p_ref[...], hi_ref[...], ((1,), (1,)))
     skip = chan_ref[:, 0:1]
     for b in range(blocks):
         acc = (back_rows(w, 0, rows, b, twist_ref, blocks) + skip * first[b]).astype(B16)
@@ -1862,8 +1869,9 @@
         [meta, lengths, keep0, near, tie(far, ga), middle, cotangent, norm2_gain],
         [row_f32, row_b16, shape((8, model), F32)],
     )
-    g_mid = gather_four(gx)
+    g_far, g_near = swap(gx, "rep", 2), swap(gx, "rep", 1)
     m3, m1, m2, m0 = call(partial(rows_kernel, 1), "mlp_rows", [tie(act, gx), full_ud], sums_shapes)
+    g_mid = [gx, g_near, g_far, swap(tie(g_far, m3), "rep", 1)]
     gy, gate_first, gmix = call(
         grad_gate_kernel,
         "grad_gate",

time: 281 us -> 279 us (level)
    ppermute x47, waiting for transfers between devices: 58.6 us -> 61.5 us  [swap(): return lax.ppermute(values, axis_name, [(i, i ^ bit) for i in range(size)])]
  transfers between devices with their start and end apart: 68 -> 68, of which waited for: 26 -> 30; matrix products, arithmetic and copies ran while one was open for 0% -> 0% of each run, Pallas kernels for 18% -> 18%
where the time goes in v1:
time: 279 us; the launch traced here: 277 us
  waiting for transfers between devices  80.4 us (29%)
  starting transfers between devices  73.1 us (26%)
  Pallas kernels  61.6 us (22%)
  blocking collectives  47.1 us (17%)
  local copies, waits for them, and re-layouts  12.6 us (5%)
    pallas_call x46, Pallas kernels, call(): pl.pallas_call(body, out_shape=outs, in_specs=[space(i, a) for i, a in en...  61.6 us
    ppermute x47, waiting for transfers between devices, swap(): return lax.ppermute(values, axis_name, [(i, i ^ bit) for i in range(size)])  61.5 us
    all_to_all x3, blocking collectives, exchange(): return lax.all_to_all(blocks, 'seq', 0, 0, tiled=True)  47.1 us
    ppermute x47, starting transfers between devices, swap(): return lax.ppermute(values, axis_name, [(i, i ^ bit) for i in range(size)])  31.3 us
    ppermute x1, starting transfers between devices, per_device_fast(): lax.ppermute(tie(gate_first, received), 'seq', [(i, (i + 7) % 8) for i in...  13.4 us
    ppermute x8, starting transfers between devices, send(): lax.ppermute(right, 'seq', BACK)  12.3 us
    unnamed x202, local copies, waits for them, and re-layouts  11.9 us
    ppermute x8, waiting for transfers between devices, send(): lax.ppermute(left, 'seq', AHEAD)  7.14 us
  transfers between devices with their start and end apart: 68, of which 30 were waited for; matrix products, arithmetic and copies ran while one was open for 0% of the time, Pallas kernels for 18%

profile of v1, /device:TPU:0, one launch (start us, length us, event | category | flops | bytes accessed | tf_op | source)
XLA Modules:
  0.0 277.0 jit_solution(14484531489098250050)
XLA Ops:
  0.8 2.2 start.1
  3.0 3.0 %collective-permute-start.6 = (bf16[128,1024]{1,0:T(8,128)(2,1)}, bf16[128,1024]{1,0:T(8,128)(2,1)S(1)}, u32[]{:S(2)}, u32[]{:S(2)}) collective-permute-start(bf16[128,1024]{1,0:T(8,128)(2,1)} %get-tuple-element.212.refs_9_), channel_id=1, source_target_pairs={{8,0},{16,8},{24,16},{28,24},{20,28},{12,20},{4,12},{0,4},{9,1},{1... | collective-permute-start | bytes 786440 | tf_op jit(solution)/shard_map/ppermute | solution.py:1633
  16.1 5.0 %filter_ahead.1 = (f32[128,1024]{1,0:T(8,128)S(1)}, f32[3,64,2048]{2,1,0:T(8,128)S(1)}, f32[3,64,2048]{2,1,0:T(8,128)S(1)}) custom-call(f32[32,2]{1,0:T(8,128)S(1)} %get-tuple-element.215.refs_0_.refs_4_.refs_5_, f32[33,64]{1,0:T(8,128)S(1)} %get-tuple-element.216.refs_1_.refs_5_, f32[64,4]{1,0:T(8,128)S(1)} %get-tuple-element.218.refs_2_.refs_8_, ...), custom_call_target="tpu_custom_call" | custom-call | flops 6000000000 | bytes 100000 | tf_op jit(solution)/shard_map/filter_ahead/pallas_call | solution.py:966
  24.4 4.3 %collective-permute-done.9.refs_0_.refs_14_ = bf16[128,1024]{1,0:T(8,128)(2,1)S(1)} collective-permute-done((bf16[128,1024]{1,0:T(8,128)(2,1)S(1)}, bf16[128,1024]{1,0:T(8,128)(2,1)S(1)}, u32[]{:S(2)}, u32[]{:S(2)}) %collective-permute-start.9) | collective-permute-done | bytes 262176 | tf_op jit(solution)/shard_map/ppermute | solution.py:1633
  33.6 3.2 %collective-permute-start.4 = (bf16[16,1024]{1,0:T(8,128)(2,1)S(1)}, bf16[16,1024]{1,0:T(8,128)(2,1)S(1)}, u32[]{:S(2)}, u32[]{:S(2)}) collective-permute-start(bf16[16,1024]{1,0:T(8,128)(2,1)S(1)} %get-tuple-element.210), channel_id=1, source_target_pairs={{0,28},{4,0},{8,4},{12,8},{16,12},{20,16},{24,20},{28,24},{1,29},{... | collective-permute-start | bytes 98312 | tf_op jit(solution)/shard_map/ppermute | solution.py:1805
  43.7 3.4 %project.1 = (bf16[8,128,1024]{2,1,0:T(8,128)(2,1)S(1)}, bf16[3,256,512]{2,1,0:T(8,128)(2,1)S(1)}, bf16[3,256,256]{2,1,0:T(8,128)(2,1)S(1)}, bf16[256,512]{1,0:T(8,128)(2,1)S(1)}) custom-call(s32[34]{0:T(128)S(1)} %dynamic-slice_bitcast_fusion.refs_0_, s32[2]{0:T(128)S(1)} %copy-done.71, bf16[128,1024]{1,0:T(8,128)(2,1)S(1)} %copy-done.2, ...), custom_call_target="tpu_custom_call" | custom-call | flops 1000000 | bytes 100000 | tf_op jit(solution)/shard_map/project/pallas_call | solution.py:966
  47.1 16.1 %all_to_all.20.refs_5_ = bf16[8,32,512]{2,1,0:T(8,128)(2,1)S(1)} all-to-all(bf16[8,32,512]{2,1,0:T(8,128)(2,1)S(1)} %bitcast.26), channel_id=1, replica_groups=mesh['seq'=8,'rep'=4] {'seq'}, dimensions={0} | all-to-all | bytes 524288 | tf_op jit(solution)/shard_map/all_to_all | solution.py:1707
  63.2 2.9 %conv_ahead.1 = (bf16[8,32,512]{2,1,0:T(8,128)(2,1)S(1)}, f32[256,1024]{1,0:T(8,128)S(1)}) custom-call(f32[128,1024]{1,0:T(8,128)S(1)} %get-tuple-element.220.refs_0_.refs_1_, f32[4,4,2,512]{3,2,1,0:T(2,128)S(1)} %copy-done.42, bf16[1024,1024]{1,0:T(8,128)(2,1)S(1)} %copy-done.1, bf16[1024,1024]{1,0:T(8,128)(2,1)S(1)} %copy-done, ...), custom_call_target="tpu_custom_call" | custom-call | flops 1000000 | bytes 100000 | tf_op jit(solution)/shard_map/conv_ahead/pallas_call | solution.py:966
  68.2 10.6 %all_to_all.21 = bf16[8,32,512]{2,1,0:T(8,128)(2,1)S(1)} all-to-all(bf16[8,32,512]{2,1,0:T(8,128)(2,1)S(1)} %get-tuple-element.233), channel_id=1, replica_groups=mesh['seq'=8,'rep'=4] {'seq'}, dimensions={0} | all-to-all | bytes 524288 | tf_op jit(solution)/shard_map/all_to_all | solution.py:1707
  84.8 7.1 %collective-permute-done.15.refs_3_ = bf16[128,1024]{1,0:T(8,128)(2,1)S(1)} collective-permute-done((bf16[128,1024]{1,0:T(8,128)(2,1)S(1)}, bf16[128,1024]{1,0:T(8,128)(2,1)S(1)}, u32[]{:S(2)}, u32[]{:S(2)}) %collective-permute-start.15) | collective-permute-done | bytes 262176 | tf_op jit(solution)/shard_map/ppermute | solution.py:23
  97.7 4.9 %collective-permute-done.17.refs_2_.refs_3_ = bf16[128,1024]{1,0:T(8,128)(2,1)S(1)} collective-permute-done((bf16[128,1024]{1,0:T(8,128)(2,1)S(1)}, bf16[128,1024]{1,0:T(8,128)(2,1)S(1)}, u32[]{:S(2)}, u32[]{:S(2)}) %collective-permute-start.17) | collective-permute-done | bytes 262176 | tf_op jit(solution)/shard_map/ppermute | solution.py:23
  105.1 3.1 %mlp.1 = (bf16[512,1024]{1,0:T(8,128)(2,1)S(1)}, bf16[512,1024]{1,0:T(8,128)(2,1)S(1)}, f32[1,1024]{1,0:T(1,128)S(1)}) custom-call(bf16[128,1024]{1,0:T(8,128)(2,1)S(1)} %get-tuple-element.238.refs_0_.refs_1_, bf16[128,1024]{1,0:T(8,128)(2,1)S(1)} %collective-permute-done.16.refs_1_.refs_2_, bf16[128,1024]{1,0:T(8,128)(2,1)S(1)} %collective-permute-done.17.refs_2_.refs_3_, ...), custom_call_target="tpu_custom_call" | custom-call | flops 1000000 | bytes 100000 | tf_op jit(solution)/shard_map/mlp/pallas_call | solution.py:966
  112.7 3.4 %mlp_grad.1 = (bf16[2,2,2,256,1024]{4,3,2,1,0:T(8,128)(2,1)S(1)}, bf16[2,2,128,1024]{3,2,1,0:T(8,128)(2,1)S(1)}, bf16[2,2,128,1024]{3,2,1,0:T(8,128)(2,1)S(1)}) custom-call(s32[34]{0:T(128)S(1)} %dynamic-slice_bitcast_fusion.refs_0_, bf16[128,1024]{1,0:T(8,128)(2,1)S(1)} %get-tuple-element.238.refs_0_.refs_1_, ...), custom_call_target="tpu_custom_call" | custom-call | flops 1000000 | bytes 100000 | tf_op jit(solution)/shard_map/mlp_grad/pallas_call | solution.py:966
  116.1 3.4 %collective-permute-done.32.refs_4_ = bf16[128,1024]{1,0:T(8,128)(2,1)S(1)} collective-permute-done((bf16[128,1024]{1,0:T(8,128)(2,1)S(1)}, bf16[128,1024]{1,0:T(8,128)(2,1)S(1)}, u32[]{:S(2)}, u32[]{:S(2)}) %collective-permute-start.32) | collective-permute-done | bytes 262176 | tf_op jit(solution)/shard_map/ppermute | solution.py:23
  126.7 2.1 collective-permute-done.35.refs_4_.refs_3_
  131.7 20.4 %all_to_all.22.refs_6_ = bf16[8,32,512]{2,1,0:T(8,128)(2,1)S(1)} all-to-all(bf16[8,32,512]{2,1,0:T(8,128)(2,1)S(1)} %bitcast.27), channel_id=1, replica_groups=mesh['seq'=8,'rep'=4] {'seq'}, dimensions={0} | all-to-all | bytes 524288 | tf_op jit(solution)/shard_map/all_to_all | solution.py:1707
  152.1 13.4 %collective-permute-start.37 = (f32[256,128]{1,0:T(8,128)S(1)}, f32[256,128]{1,0:T(8,128)S(1)}, u32[]{:S(2)}, u32[]{:S(2)}) collective-permute-start(f32[256,128]{1,0:T(8,128)S(1)} %get-tuple-element.278), channel_id=1, source_target_pairs={{0,28},{4,0},{8,4},{12,8},{16,12},{20,16},{24,20},{28,24},{1,29},{... | collective-permute-start | bytes 393224 | tf_op jit(solution)/shard_map/ppermute | solution.py:1884
  169.3 3.6 %conv_back.1 = (bf16[8,32,512]{2,1,0:T(8,128)(2,1)S(1)}, f32[4,32,512]{2,1,0:T(8,128)S(1)}) custom-call(f32[256,1024]{1,0:T(8,128)S(1)} %get-tuple-element.279.refs_0_, f32[128,1024]{1,0:T(8,128)S(1)} %get-tuple-element.220.refs_0_.refs_1_, f32[4,4,2,512]{3,2,1,0:T(2,128)S(1)} %copy-done.42, bf16[1024,1024]{1,0:T(8,128)(2,1)S(1)} %copy-done.1, ...), custom_call_target="tpu_custom_call" | custom-call | flops 1000000 | bytes 100000 | tf_op jit(solution)/shard_map/conv_back/pallas_call | solution.py:966
  175.0 4.2 %all-to-all-start.3 = ((bf16[8,32,512]{2,1,0:T(8,128)(2,1)}), bf16[8,32,512]{2,1,0:T(8,128)(2,1)}, u32[]{:S(2)}, u32[]{:S(2)}) async-start(bf16[8,32,512]{2,1,0:T(8,128)(2,1)} %copy-done.52), calls=%async_computation.3 | async-start | bytes 524288 | tf_op jit(solution)/shard_map/all_to_all | solution.py:1707
  181.4 6.1 %all-to-all-done.3 = bf16[8,32,512]{2,1,0:T(8,128)(2,1)} async-done(((bf16[8,32,512]{2,1,0:T(8,128)(2,1)}), bf16[8,32,512]{2,1,0:T(8,128)(2,1)}, u32[]{:S(2)}, u32[]{:S(2)}) %all-to-all-start.3) | async-done | bytes 262176 | tf_op jit(solution)/shard_map/all_to_all | solution.py:1707
  195.0 2.7 grad_first.1
  200.3 5.6 %grad_short.1 = (bf16[4,128,512]{2,1,0:T(8,128)(2,1)S(1)}, f32[16,256]{1,0:T(8,128)S(1)}, f32[2,1024]{1,0:T(2,128)S(1)}, bf16[128,1024]{1,0:T(8,128)(2,1)S(1)}, ...) custom-call(s32[34]{0:T(128)S(1)} %dynamic-slice_bitcast_fusion.refs_0_, ...), custom_call_target="tpu_custom_call" | custom-call | flops 1000000 | bytes 100000 | tf_op jit(solution)/shard_map/grad_short/pallas_call | solution.py:966
  215.1 6.2 %collective-permute-done.53.refs_1_ = bf16[128,1024]{1,0:T(8,128)(2,1)S(1)} collective-permute-done((bf16[128,1024]{1,0:T(8,128)(2,1)S(1)}, bf16[128,1024]{1,0:T(8,128)(2,1)S(1)}, u32[]{:S(2)}, u32[]{:S(2)}) %collective-permute-start.53) | collective-permute-done | bytes 262176 | tf_op jit(solution)/shard_map/ppermute | solution.py:23
  222.8 3.5 %filter_back.1 = (f32[64,256]{1,0:T(8,128)S(1)}, f32[64,256]{1,0:T(8,128)S(1)}) custom-call(s32[34]{0:T(128)S(1)} %dynamic-slice_bitcast_fusion.refs_0_, f32[4,32,512]{2,1,0:T(8,128)S(1)} %copy-done.46, f32[33,2048]{1,0:T(8,128)S(1)} %copy-done.41, f32[1,2048]{1,0:T(1,128)S(1)} %copy-done.74, f32[32,2]{1,0:T(8,128)S(1)} %copy-done.56, ...), custom_call_target="tpu_custom_call" | custom-call | flops 1000000 | bytes 100000 | tf_op jit(solution)/shard_map/filter_back/pallas_call | solution.py:966
  226.3 3.1 %collective-permute-done.51.refs_3_ = bf16[2,64,512]{2,1,0:T(8,128)(2,1)S(1)} collective-permute-done((bf16[2,64,512]{2,1,0:T(8,128)(2,1)S(1)}, bf16[2,64,512]{2,1,0:T(8,128)(2,1)S(1)}, u32[]{:S(2)}, u32[]{:S(2)}) %collective-permute-start.51) | collective-permute-done | bytes 131104 | tf_op jit(solution)/shard_map/ppermute | solution.py:23
  236.0 2.5 collective-permute-done.55.refs_4_
  240.7 3.2 %collective-permute-start.61 = (bf16[64,512]{1,0:T(8,128)(2,1)S(1)}, bf16[64,512]{1,0:T(8,128)(2,1)S(1)}, u32[]{:S(2)}, u32[]{:S(2)}) collective-permute-start(bf16[64,512]{1,0:T(8,128)(2,1)S(1)} %get-tuple-element.358), channel_id=1, source_target_pairs={{0,16},{4,20},{8,24},{12,28},{16,0},{20,4},{24,8},{28,12},{1,17},{... | collective-permute-start | bytes 196616 | tf_op jit(solution)/shard_map/ppermute | solution.py:23
  243.9 3.2 %collective-permute-done.61.refs_3_ = bf16[64,512]{1,0:T(8,128)(2,1)S(1)} collective-permute-done((bf16[64,512]{1,0:T(8,128)(2,1)S(1)}, bf16[64,512]{1,0:T(8,128)(2,1)S(1)}, u32[]{:S(2)}, u32[]{:S(2)}) %collective-permute-start.61) | collective-permute-done | bytes 65568 | tf_op jit(solution)/shard_map/ppermute | solution.py:23
  247.1 4.7 %collective-permute-done.60.refs_2_ = bf16[64,512]{1,0:T(8,128)(2,1)S(1)} collective-permute-done((bf16[64,512]{1,0:T(8,128)(2,1)S(1)}, bf16[64,512]{1,0:T(8,128)(2,1)S(1)}, u32[]{:S(2)}, u32[]{:S(2)}) %collective-permute-start.60) | collective-permute-done | bytes 65568 | tf_op jit(solution)/shard_map/ppermute | solution.py:23
  253.3 2.8 %collective-permute-start.64 = (bf16[64,512]{1,0:T(8,128)(2,1)S(1)}, bf16[64,512]{1,0:T(8,128)(2,1)S(1)}, u32[]{:S(2)}, u32[]{:S(2)}) collective-permute-start(bf16[64,512]{1,0:T(8,128)(2,1)S(1)} %get-tuple-element.365), channel_id=1, source_target_pairs={{0,16},{4,20},{8,24},{12,28},{16,0},{20,4},{24,8},{28,12},{1,17},{... | collective-permute-start | bytes 196616 | tf_op jit(solution)/shard_map/ppermute | solution.py:23
  256.2 10.0 %collective-permute-done.64.refs_3_ = bf16[64,512]{1,0:T(8,128)(2,1)S(1)} collective-permute-done((bf16[64,512]{1,0:T(8,128)(2,1)S(1)}, bf16[64,512]{1,0:T(8,128)(2,1)S(1)}, u32[]{:S(2)}, u32[]{:S(2)}) %collective-permute-start.64) | collective-permute-done | bytes 65568 | tf_op jit(solution)/shard_map/ppermute | solution.py:23
  269.1 4.1 %collective-permute-done.65.refs_2_ = f32[176,256]{1,0:T(8,128)S(1)} collective-permute-done((f32[176,256]{1,0:T(8,128)S(1)}, f32[176,256]{1,0:T(8,128)S(1)}, u32[]{:S(2)}, u32[]{:S(2)}) %collective-permute-start.65) | collective-permute-done | bytes 180256 | tf_op jit(solution)/shard_map/ppermute | solution.py:23
  (356 shorter events, 100.8 us)
Async XLA Ops:
  3.0 9.6 %collective-permute-start.6 = (bf16[128,1024]{1,0:T(8,128)(2,1)}, bf16[128,1024]{1,0:T(8,128)(2,1)S(1)}, u32[]{:S(2)}, u32[]{:S(2)}) collective-permute-start(bf16[128,1024]{1,0:T(8,128)(2,1)} %get-tuple-element.212.refs_9_), channel_id=1, source_target_pairs={{8,0},{16,8},{24,16},{28,24},{20,28},{12,20},{4,12},{0,4},{9,1},{1... | collective-permute-start | bytes 786440 | tf_op jit(solution)/shard_map/ppermute | solution.py:1633
  6.1 16.2 %collective-permute-start.1 = (bf16[128,1024]{1,0:T(8,128)(2,1)}, bf16[128,1024]{1,0:T(8,128)(2,1)S(1)}, u32[]{:S(2)}, u32[]{:S(2)}) collective-permute-start(bf16[128,1024]{1,0:T(8,128)(2,1)} %get-tuple-element.311.refs_1_.refs_2_.refs_6_.refs_8_), channel_id=1, source_target_pairs={{0,2},{1,3},{2,0},{3,1},{4,6},{5,7},{6,4},{7,5},{8,10},{9,11},{10,... | collective-permute-start | bytes 786440 | tf_op jit(solution)/shard_map/ppermute | solution.py:23
  29.3 9.5 %collective-permute-start.11 = (bf16[64,1024]{1,0:T(8,128)(2,1)S(1)}, bf16[64,1024]{1,0:T(8,128)(2,1)S(1)}, u32[]{:S(2)}, u32[]{:S(2)}) collective-permute-start(bf16[64,1024]{1,0:T(8,128)(2,1)S(1)} %get-tuple-element.225), channel_id=1, source_target_pairs={{0,8},{8,16},{16,24},{24,28},{28,20},{20,12},{12,4},{4,0},{1,9},{9... | collective-permute-start | bytes 393224 | tf_op jit(solution)/shard_map/ppermute | solution.py:1633
  38.8 27.3 %collective-permute-start.23 = (bf16[2,128,1024]{2,1,0:T(8,128)(2,1)S(1)}, bf16[2,128,1024]{2,1,0:T(8,128)(2,1)S(1)}, u32[]{:S(2)}, u32[]{:S(2)}) collective-permute-start(bf16[2,128,1024]{2,1,0:T(8,128)(2,1)S(1)} %get-tuple-element.242.refs_1_), channel_id=1, source_target_pairs={{8,0},{16,8},{24,16},{28,24},{20,28},{12,20},{4,12},{0,4},{9,1},{1... | collective-permute-start | bytes 1572872 | tf_op jit(solution)/shard_map/ppermute | solution.py:1633
  40.3 25.8 %collective-permute-start.22 = (bf16[2,128,1024]{2,1,0:T(8,128)(2,1)S(1)}, bf16[2,128,1024]{2,1,0:T(8,128)(2,1)S(1)}, u32[]{:S(2)}, u32[]{:S(2)}) collective-permute-start(bf16[2,128,1024]{2,1,0:T(8,128)(2,1)S(1)} %get-tuple-element.242.refs_1_), channel_id=1, source_target_pairs={{0,8},{8,16},{16,24},{24,28},{28,20},{20,12},{12,4},{4,0},{1,9},{9... | collective-permute-start | bytes 1572872 | tf_op jit(solution)/shard_map/ppermute | solution.py:1633
  66.1 14.4 %collective-permute-start.24 = (bf16[2,128,1024]{2,1,0:T(8,128)(2,1)S(1)}, bf16[2,128,1024]{2,1,0:T(8,128)(2,1)S(1)}, u32[]{:S(2)}, u32[]{:S(2)}) collective-permute-start(bf16[2,128,1024]{2,1,0:T(8,128)(2,1)S(1)} %collective-permute-done.22.refs_2_), channel_id=1, source_target_pairs={{0,8},{8,16},{16,24},{24,28},{28,20},{20,12},{12,4},{4,0},{1,9},{9... | collective-permute-start | bytes 1572872 | tf_op jit(solution)/shard_map/ppermute | solution.py:1633
  66.2 14.3 %collective-permute-start.25 = (bf16[2,128,1024]{2,1,0:T(8,128)(2,1)S(1)}, bf16[2,128,1024]{2,1,0:T(8,128)(2,1)S(1)}, u32[]{:S(2)}, u32[]{:S(2)}) collective-permute-start(bf16[2,128,1024]{2,1,0:T(8,128)(2,1)S(1)} %collective-permute-done.23.refs_3_), channel_id=1, source_target_pairs={{8,0},{16,8},{24,16},{28,24},{20,28},{12,20},{4,12},{0,4},{9,1},{1... | collective-permute-start | bytes 1572872 | tf_op jit(solution)/shard_map/ppermute | solution.py:1633
  80.5 14.3 %collective-permute-start.26 = (bf16[2,128,1024]{2,1,0:T(8,128)(2,1)S(1)}, bf16[2,128,1024]{2,1,0:T(8,128)(2,1)S(1)}, u32[]{:S(2)}, u32[]{:S(2)}) collective-permute-start(bf16[2,128,1024]{2,1,0:T(8,128)(2,1)S(1)} %collective-permute-done.24.refs_4_), channel_id=1, source_target_pairs={{0,8},{8,16},{16,24},{24,28},{28,20},{20,12},{12,4},{4,0},{1,9},{9... | collective-permute-start | bytes 1572872 | tf_op jit(solution)/shard_map/ppermute | solution.py:1633
  80.7 14.4 %collective-permute-start.27 = (bf16[2,128,1024]{2,1,0:T(8,128)(2,1)S(1)}, bf16[2,128,1024]{2,1,0:T(8,128)(2,1)S(1)}, u32[]{:S(2)}, u32[]{:S(2)}) collective-permute-start(bf16[2,128,1024]{2,1,0:T(8,128)(2,1)S(1)} %collective-permute-done.25.refs_5_), channel_id=1, source_target_pairs={{8,0},{16,8},{24,16},{28,24},{20,28},{12,20},{4,12},{0,4},{9,1},{1... | collective-permute-start | bytes 1572872 | tf_op jit(solution)/shard_map/ppermute | solution.py:1633
  84.3 13.2 %collective-permute-start.20 = (bf16[128,1024]{1,0:T(8,128)(2,1)S(1)}, bf16[128,1024]{1,0:T(8,128)(2,1)S(1)}, u32[]{:S(2)}, u32[]{:S(2)}) collective-permute-start(bf16[128,1024]{1,0:T(8,128)(2,1)S(1)} %get-tuple-element.240.refs_4_.refs_5_), channel_id=1, source_target_pairs={{0,2},{1,3},{2,0},{3,1},{4,6},{5,7},{6,4},{7,5},{8,10},{9,11},{10,... | collective-permute-start | bytes 786440 | tf_op jit(solution)/shard_map/ppermute | solution.py:23
  92.2 10.5 %collective-permute-start.17 = (bf16[128,1024]{1,0:T(8,128)(2,1)S(1)}, bf16[128,1024]{1,0:T(8,128)(2,1)S(1)}, u32[]{:S(2)}, u32[]{:S(2)}) collective-permute-start(bf16[128,1024]{1,0:T(8,128)(2,1)S(1)} %get-tuple-element.238.refs_0_.refs_1_), channel_id=1, source_target_pairs={{0,2},{1,3},{2,0},{3,1},{4,6},{5,7},{6,4},{7,5},{8,10},{9,11},{10,... | collective-permute-start | bytes 786440 | tf_op jit(solution)/shard_map/ppermute | solution.py:23
  122.9 42.6 %collective-permute-start.39 = (bf16[2,2,128,1024]{3,2,1,0:T(8,128)(2,1)S(1)}, bf16[2,2,128,1024]{3,2,1,0:T(8,128)(2,1)S(1)}, u32[]{:S(2)}, u32[]{:S(2)}) collective-permute-start(bf16[2,2,128,1024]{3,2,1,0:T(8,128)(2,1)S(1)} %get-tuple-element.281), channel_id=1, source_target_pairs={{0,8},{4,12},{8,0},{12,4},{16,24},{20,28},{24,16},{28,20},{1,9},{5... | collective-permute-start | bytes 3145736 | tf_op jit(solution)/shard_map/ppermute | solution.py:23
  123.8 41.7 %collective-permute-start.38 = (bf16[2,2,128,1024]{3,2,1,0:T(8,128)(2,1)S(1)}, bf16[2,2,128,1024]{3,2,1,0:T(8,128)(2,1)S(1)}, u32[]{:S(2)}, u32[]{:S(2)}) collective-permute-start(bf16[2,2,128,1024]{3,2,1,0:T(8,128)(2,1)S(1)} %get-tuple-element.261), channel_id=1, source_target_pairs={{0,4},{4,0},{8,12},{12,8},{16,20},{20,16},{24,28},{28,24},{1,5},{5... | collective-permute-start | bytes 3145736 | tf_op jit(solution)/shard_map/ppermute | solution.py:23
  152.1 22.3 %collective-permute-start.37 = (f32[256,128]{1,0:T(8,128)S(1)}, f32[256,128]{1,0:T(8,128)S(1)}, u32[]{:S(2)}, u32[]{:S(2)}) collective-permute-start(f32[256,128]{1,0:T(8,128)S(1)} %get-tuple-element.278), channel_id=1, source_target_pairs={{0,28},{4,0},{8,4},{12,8},{16,12},{20,16},{24,20},{28,24},{1,29},{... | collective-permute-start | bytes 393224 | tf_op jit(solution)/shard_map/ppermute | solution.py:1884
  168.2 12.0 %collective-permute-start.41 = (bf16[2,128,1024]{2,1,0:T(8,128)(2,1)}, bf16[2,128,1024]{2,1,0:T(8,128)(2,1)}, u32[]{:S(2)}, u32[]{:S(2)}) collective-permute-start(bf16[2,128,1024]{2,1,0:T(8,128)(2,1)} %get-tuple-element.290), channel_id=1, source_target_pairs={{0,4},{4,0},{8,12},{12,8},{16,20},{20,16},{24,28},{28,24},{1,5},{5... | collective-permute-start | bytes 1572872 | tf_op jit(solution)/shard_map/ppermute | solution.py:23
  168.4 13.0 %collective-permute-start.40 = (bf16[2,128,1024]{2,1,0:T(8,128)(2,1)}, bf16[2,128,1024]{2,1,0:T(8,128)(2,1)}, u32[]{:S(2)}, u32[]{:S(2)}) collective-permute-start(bf16[2,128,1024]{2,1,0:T(8,128)(2,1)} %get-tuple-element.284), channel_id=1, source_target_pairs={{0,8},{4,12},{8,0},{12,4},{16,24},{20,28},{24,16},{28,20},{1,9},{5... | collective-permute-start | bytes 1572872 | tf_op jit(solution)/shard_map/ppermute | solution.py:23
  175.0 12.5 %all-to-all-start.3 = ((bf16[8,32,512]{2,1,0:T(8,128)(2,1)}), bf16[8,32,512]{2,1,0:T(8,128)(2,1)}, u32[]{:S(2)}, u32[]{:S(2)}) async-start(bf16[8,32,512]{2,1,0:T(8,128)(2,1)} %copy-done.52), calls=%async_computation.3 | async-start | bytes 524288 | tf_op jit(solution)/shard_map/all_to_all | solution.py:1707
  194.2 13.6 %collective-permute-start.45 = (bf16[128,1024]{1,0:T(8,128)(2,1)S(1)}, bf16[128,1024]{1,0:T(8,128)(2,1)S(1)}, u32[]{:S(2)}, u32[]{:S(2)}) collective-permute-start(bf16[128,1024]{1,0:T(8,128)(2,1)S(1)} %get-tuple-element.293), channel_id=1, source_target_pairs={{0,16},{4,20},{8,24},{12,28},{16,0},{20,4},{24,8},{28,12},{1,17},{... | collective-permute-start | bytes 786440 | tf_op jit(solution)/shard_map/ppermute | solution.py:23
  199.3 9.3 %collective-permute-start.44 = (bf16[2,2,64,512]{3,2,1,0:T(8,128)(2,1)S(1)}, bf16[2,2,64,512]{3,2,1,0:T(8,128)(2,1)S(1)}, u32[]{:S(2)}, u32[]{:S(2)}) collective-permute-start(bf16[2,2,64,512]{3,2,1,0:T(8,128)(2,1)S(1)} %get-tuple-element.303), channel_id=1, source_target_pairs={{0,8},{4,12},{8,0},{12,4},{16,24},{20,28},{24,16},{28,20},{1,9},{5... | collective-permute-start | bytes 786440 | tf_op jit(solution)/shard_map/ppermute | solution.py:23
  206.0 15.3 %collective-permute-start.53 = (bf16[128,1024]{1,0:T(8,128)(2,1)S(1)}, bf16[128,1024]{1,0:T(8,128)(2,1)S(1)}, u32[]{:S(2)}, u32[]{:S(2)}) collective-permute-start(bf16[128,1024]{1,0:T(8,128)(2,1)S(1)} %get-tuple-element.326), channel_id=1, source_target_pairs={{0,16},{4,20},{8,24},{12,28},{16,0},{20,4},{24,8},{28,12},{1,17},{... | collective-permute-start | bytes 786440 | tf_op jit(solution)/shard_map/ppermute | solution.py:23
  209.4 13.1 %collective-permute-start.52 = (bf16[2,64,512]{2,1,0:T(8,128)(2,1)S(1)}, bf16[2,64,512]{2,1,0:T(8,128)(2,1)S(1)}, u32[]{:S(2)}, u32[]{:S(2)}) collective-permute-start(bf16[2,64,512]{2,1,0:T(8,128)(2,1)S(1)} %get-tuple-element.323), channel_id=1, source_target_pairs={{0,4},{4,0},{8,12},{12,8},{16,20},{20,16},{24,28},{28,24},{1,5},{5... | collective-permute-start | bytes 393224 | tf_op jit(solution)/shard_map/ppermute | solution.py:23
  211.1 19.8 %collective-permute-start.49 = (bf16[128,1024]{1,0:T(8,128)(2,1)S(1)}, bf16[128,1024]{1,0:T(8,128)(2,1)S(1)}, u32[]{:S(2)}, u32[]{:S(2)}) collective-permute-start(bf16[128,1024]{1,0:T(8,128)(2,1)S(1)} %get-tuple-element.320), channel_id=1, source_target_pairs={{0,1},{1,0},{2,3},{3,2},{4,5},{5,4},{6,7},{7,6},{8,9},{9,8},{10,11... | collective-permute-start | bytes 786440 | tf_op jit(solution)/shard_map/ppermute | solution.py:23
  211.2 19.7 %collective-permute-start.50 = (bf16[128,1024]{1,0:T(8,128)(2,1)S(1)}, bf16[128,1024]{1,0:T(8,128)(2,1)S(1)}, u32[]{:S(2)}, u32[]{:S(2)}) collective-permute-start(bf16[128,1024]{1,0:T(8,128)(2,1)S(1)} %add_far.6), channel_id=1, source_target_pairs={{0,2},{1,3},{2,0},{3,1},{4,6},{5,7},{6,4},{7,5},{8,10},{9,11},{10,... | collective-permute-start | bytes 786440 | tf_op jit(solution)/shard_map/ppermute | solution.py:23
  213.1 19.1 %collective-permute-start.48 = (bf16[2,2,64,512]{3,2,1,0:T(8,128)(2,1)S(1)}, bf16[2,2,64,512]{3,2,1,0:T(8,128)(2,1)S(1)}, u32[]{:S(2)}, u32[]{:S(2)}) collective-permute-start(bf16[2,2,64,512]{3,2,1,0:T(8,128)(2,1)S(1)} %get-tuple-element.318), channel_id=1, source_target_pairs={{0,8},{4,12},{8,0},{12,4},{16,24},{20,28},{24,16},{28,20},{1,9},{5... | collective-permute-start | bytes 786440 | tf_op jit(solution)/shard_map/ppermute | solution.py:23
  221.4 10.8 %collective-permute-start.47 = (bf16[2,2,64,512]{3,2,1,0:T(8,128)(2,1)S(1)}, bf16[2,2,64,512]{3,2,1,0:T(8,128)(2,1)S(1)}, u32[]{:S(2)}, u32[]{:S(2)}) collective-permute-start(bf16[2,2,64,512]{3,2,1,0:T(8,128)(2,1)S(1)} %get-tuple-element.317), channel_id=1, source_target_pairs={{0,4},{4,0},{8,12},{12,8},{16,20},{20,16},{24,28},{28,24},{1,5},{5... | collective-permute-start | bytes 786440 | tf_op jit(solution)/shard_map/ppermute | solution.py:23
  240.5 11.9 %collective-permute-start.57 = (bf16[128,1024]{1,0:T(8,128)(2,1)S(1)}, bf16[128,1024]{1,0:T(8,128)(2,1)S(1)}, u32[]{:S(2)}, u32[]{:S(2)}) collective-permute-start(bf16[128,1024]{1,0:T(8,128)(2,1)S(1)} %copy-done.89), channel_id=1, source_target_pairs={{0,1},{1,0},{2,3},{3,2},{4,5},{5,4},{6,7},{7,6},{8,9},{9,8},{10,11... | collective-permute-start | bytes 786440 | tf_op jit(solution)/shard_map/ppermute | solution.py:23
  240.6 11.9 %collective-permute-start.59 = (f32[176,256]{1,0:T(8,128)S(1)}, f32[176,256]{1,0:T(8,128)S(1)}, u32[]{:S(2)}, u32[]{:S(2)}) collective-permute-start(f32[176,256]{1,0:T(8,128)S(1)} %add_small.3.refs_0_), channel_id=1, source_target_pairs={{0,8},{4,12},{8,0},{12,4},{16,24},{20,28},{24,16},{28,20},{1,9},{5... | collective-permute-start | bytes 540680 | tf_op jit(solution)/shard_map/ppermute | solution.py:23
  252.5 15.1 %collective-permute-start.62 = (f32[176,256]{1,0:T(8,128)S(1)}, f32[176,256]{1,0:T(8,128)S(1)}, u32[]{:S(2)}, u32[]{:S(2)}) collective-permute-start(f32[176,256]{1,0:T(8,128)S(1)} %add_small.4.refs_0_), channel_id=1, source_target_pairs={{0,16},{4,20},{8,24},{12,28},{16,0},{20,4},{24,8},{28,12},{1,17},{... | collective-permute-start | bytes 540680 | tf_op jit(solution)/shard_map/ppermute | solution.py:23
  252.6 15.7 %collective-permute-start.58 = (bf16[128,1024]{1,0:T(8,128)(2,1)S(1)}, bf16[128,1024]{1,0:T(8,128)(2,1)S(1)}, u32[]{:S(2)}, u32[]{:S(2)}) collective-permute-start(bf16[128,1024]{1,0:T(8,128)(2,1)S(1)} %add_far.7), channel_id=1, source_target_pairs={{0,2},{1,3},{2,0},{3,1},{4,6},{5,7},{6,4},{7,5},{8,10},{9,11},{10,... | collective-permute-start | bytes 786440 | tf_op jit(solution)/shard_map/ppermute | solution.py:23
  253.3 15.0 %collective-permute-start.33 = (bf16[128,1024]{1,0:T(8,128)(2,1)S(1)}, bf16[128,1024]{1,0:T(8,128)(2,1)S(1)}, u32[]{:S(2)}, u32[]{:S(2)}) collective-permute-start(bf16[128,1024]{1,0:T(8,128)(2,1)S(1)} %copy-done.87), channel_id=1, source_target_pairs={{0,1},{1,0},{2,3},{3,2},{4,5},{5,4},{6,7},{7,6},{8,9},{9,8},{10,11... | collective-permute-start | bytes 786440 | tf_op jit(solution)/shard_map/ppermute | solution.py:23
  253.3 12.9 %collective-permute-start.64 = (bf16[64,512]{1,0:T(8,128)(2,1)S(1)}, bf16[64,512]{1,0:T(8,128)(2,1)S(1)}, u32[]{:S(2)}, u32[]{:S(2)}) collective-permute-start(bf16[64,512]{1,0:T(8,128)(2,1)S(1)} %get-tuple-element.365), channel_id=1, source_target_pairs={{0,16},{4,20},{8,24},{12,28},{16,0},{20,4},{24,8},{28,12},{1,17},{... | collective-permute-start | bytes 196616 | tf_op jit(solution)/shard_map/ppermute | solution.py:23
  256.1 10.8 %collective-permute-start.63 = (bf16[64,512]{1,0:T(8,128)(2,1)S(1)}, bf16[64,512]{1,0:T(8,128)(2,1)S(1)}, u32[]{:S(2)}, u32[]{:S(2)}) collective-permute-start(bf16[64,512]{1,0:T(8,128)(2,1)S(1)} %get-tuple-element.354), channel_id=1, source_target_pairs={{0,16},{4,20},{8,24},{12,28},{16,0},{20,4},{24,8},{28,12},{1,17},{... | collective-permute-start | bytes 196616 | tf_op jit(solution)/shard_map/ppermute | solution.py:23
  (137 other events, 1401.2 us)
